TPU v7x, 32 devices: a whole 2x2x4 slice. The times are simulated.
32 devices in a mesh: groups: 2 (over y), row: 8 (over z, x), col: 2 (over core).
Axes of the slice: x: 2, y: 2, z: 4, core: 2. Of those that a mesh axis runs over, the one named last changes fastest.
Arguments:
- gram_old: bfloat16 [28672, 14336], P(('groups', 'row'), 'col'), parts along dimension 0, may hold values from -10 to 256, as said below
- activations: bfloat16 [256, 14336], P('groups', 'row'), parts along dimension 0, may hold values from -0.5 to 0.5
- weights: float32 [14336, 512], P('row', ('groups', 'col')), parts along dimension 1, may hold values from -6 to 6
- block_mask: int32 [112, 4], P(None, 'groups'), parts along dimension 1, may hold values 0 or 1
Outputs:
- pruned: float32 [14336, 512], P('row', ('groups', 'col')), parts along dimension 1
There are 2 independent parts, one for each index of `groups`. A program takes and returns all parts, laid end to end along the dimension named above; each array names one. Nothing has to cross between parts.
Inputs may be any that keep to these rules, and one draw needn't show every extreme that they name: `gram_old`: symmetric and positive definite.
All inputs are finite; a program needn't handle non-finite values.
Results may differ from a plain program's by a relative error of at most 0.00076.
Values may be sent and summed in bfloat16 or wider, within the bound.
No kernel may reach another device: no remote copies, remote signals or barrier semaphores. Data moves between devices by JAX's collectives and lax.ppermute only.
A program may use at most 128 MiB of HBM per device.

v0:
```python
import functools

import jax
import jax.numpy as jnp
from jax import lax
from jax.experimental import pallas as pl
from jax.experimental.pallas import tpu as pltpu
from jax.sharding import PartitionSpec as P

BLK = 128
TILES = 1
PARTS = 4
LIMIT = 8 * 1024 * 1024
AXES = ("row", "col")
WEIGHTS = ((1, 1, 0.3, 0.3, 8, 0.02, 0.02), (1, 0.02, 0.3, 2, 4, 0.3, 4))

damping_ratio = 0.3
epsilon = 1e-06


def swap(value, axis, distance):
    return lax.ppermute(value, axis, [(i, i ^ distance) for i in range(lax.axis_size(axis))])


def sum_part(value, count):
    devices = 2 * count
    unit = 1
    while unit < devices:
        size = 2 if unit == 1 else min(4, devices // unit)
        swaps = [[(i, i ^ k * unit) for i in range(devices)] for k in range(1, size)]
        value += sum(lax.ppermute(value, AXES, pairs) for pairs in swaps)
        unit *= size
    return value


def expand_local(block_mask, row_index, row_block, col_index, width_cols):
    if width_cols != BLK:
        row_ids = (row_index * row_block + jnp.arange(row_block, dtype=jnp.int32)) // BLK
        col_ids = (col_index * width_cols + jnp.arange(width_cols, dtype=jnp.int32)) // BLK
        return block_mask[row_ids][:, col_ids].astype(jnp.float32)
    piece = BLK
    while row_block % piece:
        piece //= 2
    column = lax.dynamic_index_in_dim(block_mask, col_index, 1, keepdims=False)
    column = jnp.repeat(column, BLK // piece) if piece != BLK else column
    count = row_block // piece
    own = lax.dynamic_slice_in_dim(column, row_index * count, count, 0).astype(jnp.float32)
    return jnp.broadcast_to(own[:, None, None], (count, piece, width_cols)).reshape(
        row_block, width_cols
    )


class Ring:
    def __init__(self, count):
        self.count = count
        self.order = list(range(0, count, 2)) + list(range(count - 1, 0, -2))
        self.last = count // 2 - 1

    def row(self, place):
        return self.order[place % self.count]

    def half(self, place):
        return self.row(place) * 2 // self.count

    def ahead(self, place):
        return int(place % self.count >= self.count // 2)

    def device(self, place, core):
        return self.row(place) * 2 + core

    def source(self, place, core, step):
        return place - 1 - step if core == self.ahead(place) else place + 1 + step

    def first_column(self, place, core, step):
        origin = self.ahead(self.source(place, core, step))
        return origin if core == self.ahead(place) else 1 - origin

    def places(self):
        return [(place, core) for place in range(self.count) for core in range(2)]

    def shift(self):
        pairs = []
        for place in range(self.count):
            pairs.append(
                (self.device(place, self.ahead(place)), self.device(place + 1, self.ahead(place + 1)))
            )
            pairs.append(
                (
                    self.device(place, 1 - self.ahead(place)),
                    self.device(place - 1, 1 - self.ahead(place - 1)),
                )
            )
        return pairs

    def hand_over(self, step):
        return [
            (self.device(place, core), self.device(place, 1 - core))
            for place, core in self.places()
            if self.half(self.source(place, core, step)) != core
        ]

    def slots(self):
        found = []
        for step in range(self.last):
            found.append((True, step))
            if self.hand_over(step):
                found.append((False, step))
        return found

    def loads(self, slot):
        base = 3 * (2 + len(self.slots()))
        return [base + slot + 1] if slot + 1 < self.count // 2 else []

    def entry(self, place, core, carrier, step):
        source = self.source(place, carrier, step)
        return [
            self.row(source) % (self.count // 2),
            int(self.half(source) == core),
            int(self.first_column(place, carrier, step) != core),
        ]

    def table(self):
        half = self.count // 2
        lines = [None] * (2 * self.count)
        for place, core in self.places():
            line = [self.row(place) % half, int(self.half(place) == core), 0]
            for carrier, step in self.slots():
                line += self.entry(place, core, core if carrier else 1 - core, step)
            line += self.entry(place, core, core, self.last)
            needed = [line[k] for k in range(0, len(line), 3) if line[k + 1]]
            line += needed
            lines[self.device(place, core)] = line
        return lines


def pick(ring, entry):
    device = lax.axis_index("row") * 2 + lax.axis_index("col")
    values = [line[entry] for line in ring.table()]
    picked = jnp.int32(values[0])
    for index, value in enumerate(values):
        if value != values[0]:
            picked = jnp.where(device == index, jnp.int32(value), picked)
    return picked


def block_copies(ring, load, gram, store, sems):
    rows = gram.shape[0]
    there = pl.ds(pl.multiple_of(pick(ring, load) * rows, BLK), rows)
    parts = [pl.ds(part * rows // PARTS, rows // PARTS) for part in range(PARTS)]
    return [
        pltpu.make_async_copy(gram.at[here, there], store.at[here, there], sems.at[part])
        for part, here in enumerate(parts)
    ]


def load_kernel(ring, load, gram, acts, second, store, across, passed, sems):
    copies = block_copies(ring, load, gram, store, sems)
    for copy in copies:
        copy.start()
    across[...] = acts[...].astype(jnp.float32).T.astype(across.dtype)
    for copy in copies:
        copy.wait()


def load_first(ring, gram, acts, second):
    whole = pl.BlockSpec(memory_space=pltpu.VMEM)
    return pl.pallas_call(
        functools.partial(load_kernel, ring, ring.loads(-1)[0]),
        in_specs=[pl.BlockSpec(memory_space=pltpu.HBM), whole, whole],
        out_specs=[whole] * 3,
        out_shape=[
            jax.ShapeDtypeStruct(gram.shape, gram.dtype),
            jax.ShapeDtypeStruct(acts.shape[::-1], acts.dtype),
            jax.ShapeDtypeStruct(second.shape, second.dtype),
        ],
        scratch_shapes=[pltpu.SemaphoreType.DMA((PARTS,))],
        input_output_aliases={2: 2},
        compiler_params=pltpu.CompilerParams(vmem_limit_bytes=LIMIT),
    )(gram, acts, second)


def product_kernel(ring, slot, loads, with_trace, first, second, across, *refs):
    copies = []
    if with_trace:
        acts, gram, _, own, other, store, trace, sems = refs
        trace[...] = jnp.zeros_like(trace)
    elif loads:
        gram, _, own, other, store, sems = refs[-6:]
    else:
        own, other, store = refs[-3:]
    if loads:
        copies = block_copies(ring, loads[0], gram, store, sems)
    for copy in copies:
        copy.start()
    rows, width = own.shape
    start = pl.multiple_of(pick(ring, 3 * slot) * rows, BLK)
    flip = pick(ring, 3 * slot + 2) == 1
    if slot == 0:
        own[...] = jnp.zeros_like(own)
        other[...] = jnp.zeros_like(other)

    @pl.when(pick(ring, 3 * slot + 1) == 1)
    def _():
        @pl.loop(0, TILES)
        def _(tile):
            size = rows // TILES
            here = pl.ds(pl.multiple_of(tile * size, size), size)
            lines = jnp.concatenate([store[here, pl.ds(start, rows)], across[here, :]], axis=1)
            panel = jnp.concatenate([first[...], second[...]], axis=1)
            result = jnp.dot(lines, panel, preferred_element_type=jnp.float32)
            left, right = result[:, :width], result[:, width:]
            own[here, :] += jnp.where(flip, right, left)
            other[here, :] += jnp.where(flip, left, right)

        if with_trace:
            add_diagonal(store, start, acts, trace)

    for copy in copies:
        copy.wait()


def add_diagonal(store, start, acts, trace):
    lines = lax.broadcasted_iota(jnp.int32, (BLK, BLK), 0)
    same = lines == lax.broadcasted_iota(jnp.int32, (BLK, BLK), 1)
    for block in range(acts.shape[1] // BLK):
        here = slice(block * BLK, (block + 1) * BLK)
        there = pl.ds(pl.multiple_of(start + block * BLK, BLK), BLK)
        square = store[here, there].astype(jnp.float32)
        diag = jnp.sum(jnp.where(same, square, 0.0), axis=0, keepdims=True)
        part = acts[:, here].astype(jnp.float32)
        diag += jnp.sum(part * part, axis=0, keepdims=True)
        trace[0:1, :] += diag.astype(jnp.bfloat16).astype(jnp.float32)


def product(ring, slot, loads, gram, store, message, across, acts, acc):
    rows = across.shape[0]
    width = message[0].shape[1]
    weight = WEIGHTS[gram is None][slot]
    whole = pl.BlockSpec(memory_space=pltpu.VMEM)
    with_trace = bool(loads) and slot == 0
    operands = [*message, across]
    aliases = {len(operands) + k: k for k in range(len(acc))}
    operands += acc
    in_specs = [whole] * (len(operands) + 1)
    out_shape = [jax.ShapeDtypeStruct((rows, width), jnp.float32)] * 2
    out_shape.append(jax.ShapeDtypeStruct(store.shape, store.dtype))
    scratch = []
    if with_trace:
        operands.append(acts)
        in_specs.append(whole)
        out_shape.append(jax.ShapeDtypeStruct((8, width), jnp.float32))
    aliases[len(operands) + bool(loads)] = 2
    if loads:
        operands.append(gram)
        in_specs.insert(len(operands) - 1, pl.BlockSpec(memory_space=pltpu.HBM))
        scratch = [pltpu.SemaphoreType.DMA((PARTS,))]
    operands.append(store)
    results = pl.pallas_call(
        functools.partial(product_kernel, ring, slot, loads, with_trace),
        in_specs=in_specs,
        out_specs=[whole] * len(out_shape),
        out_shape=out_shape,
        scratch_shapes=scratch,
        input_output_aliases=aliases,
        compiler_params=pltpu.CompilerParams(vmem_limit_bytes=LIMIT),
        cost_estimate=pl.CostEstimate(
            flops=int(weight * 4 * rows * rows * width),
            bytes_accessed=int(weight * 2 * rows * rows),
            transcendentals=0,
        ),
    )(*operands)
    return results[:2], results[2], results[3:]


def after(value, others):
    return lax.optimization_barrier((value, *others))[0]


def ring_apply(ring, gram, message, acts, early):
    first = message
    trace = []
    store, across, second = early(swap(message, "col", 1))
    ready = [(first, second)]
    acc = []
    slot = 0

    def work(others=()):
        nonlocal acc, store, slot, trace
        if not ready:
            return
        parts = ready.pop(0)
        parts = (after(parts[0], others), parts[1])
        loads = [] if gram is None else ring.loads(slot)
        acc, store, added = product(ring, slot, loads, gram, store, parts, across, acts, acc)
        trace = trace or added
        slot += 1

    def hand_over(step):
        if ring.hand_over(step):
            ready.append(tuple(swap(after(part, acc[:1]), "col", 1) for part in held))

    for step in range(ring.last):
        came = lax.ppermute(after(first, acc[:1]), AXES, ring.shift())
        if step:
            work([first])
        second = lax.ppermute(after(second, acc[:1]), AXES, ring.shift())
        if step:
            hand_over(step - 1)
            work()
        first = came
        held = (first, second)
        ready.append(held)
    first = lax.ppermute(after(first, acc[:1]), AXES, ring.shift())
    hand_over(ring.last - 1)
    while ready:
        work()
    last = (first, swap(after(first, acc[:1]), "col", 1))
    (own, other), store, _ = product(ring, slot, [], gram, store, last, across, acts, acc)
    return own, swap(other, "col", 1), store, trace


def put_message(message, acts, rows):
    message[rows:, :] = jnp.dot(
        acts[...], message[:rows, :], preferred_element_type=jnp.float32
    ).astype(message.dtype)


def head_kernel(weights, blocks, acts, message):
    rows = weights.shape[0]
    for block in range(rows // BLK):
        here = slice(block * BLK, (block + 1) * BLK)
        dense = weights[here, :]
        message[here, :] = (blocks[block : block + 1, :] * dense - dense).astype(message.dtype)
    put_message(message, acts, rows)


def turn_kernel(own, received, blocks, acts, _, grad, message, __):
    rows = own.shape[0]
    for block in range(rows // BLK):
        here = slice(block * BLK, (block + 1) * BLK)
        grad_first = own[here, :] + received[here, :]
        grad[here, :] = grad_first
        message[here, :] = (blocks[block : block + 1, :] * grad_first).astype(message.dtype)
    put_message(message, acts, rows)


def lane_sums(value):
    return jnp.sum(value, axis=0, keepdims=True)


def curve_kernel(trace, grad, own, received, blocks, curve_ref, sums_ref):
    rows = grad.shape[0]
    sums_ref[...] = jnp.zeros_like(sums_ref)
    sums_ref[0:1, :] = trace[0:1, :]
    for block in range(rows // BLK):
        here = slice(block * BLK, (block + 1) * BLK)
        kept = blocks[block : block + 1, :]
        curve = own[here, :] + received[here, :]
        curve_ref[here, :] = curve
        step_dir = kept * grad[here, :]
        masked = kept * curve
        sums_ref[1:2, :] += lane_sums(step_dir * step_dir)
        sums_ref[2:3, :] += lane_sums(step_dir * curve)
        sums_ref[3:4, :] += lane_sums(masked * masked)


def last_kernel(units, sums, grad, curve, weights, blocks, out_ref):
    totals = jnp.sum(sums[...], axis=1, keepdims=True)
    trace_total, grad_square = totals[0:1, :], totals[1:2, :]
    grad_curve, curve_square = totals[2:3, :], totals[3:4, :]
    damping = damping_ratio * trace_total / units
    step_first = grad_square / (grad_curve + damping * grad_square + epsilon)
    step_second = (grad_curve + damping * grad_square) / (
        curve_square + 2.0 * damping * grad_curve + damping * damping * grad_square + epsilon
    )
    rows = grad.shape[0]
    for block in range(rows // BLK):
        here = slice(block * BLK, (block + 1) * BLK)
        kept = blocks[block : block + 1, :]
        grad_first = grad[here, :]
        step_dir = kept * grad_first
        grad_second = grad_first - step_first * curve[here, :]
        out_ref[here, :] = (
            kept * weights[here, :] - step_first * step_dir - step_second * (kept * grad_second)
        )


def gather_apply(gram, activations, panel, col_index):
    half = gram.shape[1]
    full = lax.all_gather(panel, "row", axis=0, tiled=True)
    own_half = lax.dynamic_slice_in_dim(full, col_index * half, half, 0)
    need = lax.dynamic_slice_in_dim(full, (1 - col_index) * half, half, 0)
    other_half = swap(need, "col", 1)
    own = jnp.dot(gram, own_half, preferred_element_type=jnp.float32)
    partial = jnp.dot(gram, other_half, preferred_element_type=jnp.float32)
    low = lax.psum(jnp.dot(activations, panel, preferred_element_type=jnp.float32), "row")
    update = lax.dot_general(
        activations.astype(jnp.float32),
        low,
        (((0,), (0,)), ((), ())),
        precision=lax.Precision.HIGHEST,
        preferred_element_type=jnp.float32,
    )
    return own + swap(partial, "col", 1) + update


def per_device_general(gram_old, activations, weights, block_mask):
    row_block, half_width = gram_old.shape
    width_cols = weights.shape[1]
    units = lax.axis_size("row") * row_block
    row_index = lax.axis_index("row")
    col_index = lax.axis_index("col")
    mask_local = expand_local(block_mask, row_index, row_block, col_index, width_cols)
    kept_weights = mask_local * weights
    diff_low = (kept_weights - weights).astype(jnp.bfloat16)
    acts = activations.astype(jnp.float32)
    column_squares = jnp.sum(acts * acts, axis=0)
    grad_first = gather_apply(gram_old, activations, diff_low, col_index)
    place = row_index * row_block + jnp.arange(row_block, dtype=jnp.int32)
    place = place - col_index * half_width
    on_diagonal = jnp.arange(half_width, dtype=jnp.int32)[None, :] == place[:, None]
    new_gram = gram_old.astype(jnp.float32) + column_squares[:, None]
    new_gram = new_gram.astype(jnp.bfloat16).astype(jnp.float32)
    trace_part = jnp.sum(jnp.where(on_diagonal, new_gram, 0.0))
    step_dir = mask_local * grad_first
    curvature = gather_apply(gram_old, activations, step_dir.astype(jnp.bfloat16), col_index)
    masked_curve = mask_local * curvature
    sums = jnp.stack(
        [
            trace_part,
            jnp.sum(step_dir * step_dir),
            jnp.sum(step_dir * curvature),
            jnp.sum(masked_curve * masked_curve),
        ]
    )
    sums = lax.psum(sums, ("row", "col"))
    trace_total, grad_square, grad_curve, curve_square = sums[0], sums[1], sums[2], sums[3]
    damping = damping_ratio * trace_total / units
    step_first = grad_square / (grad_curve + damping * grad_square + epsilon)
    step_second = (grad_curve + damping * grad_square) / (
        curve_square + 2.0 * damping * grad_curve + damping * damping * grad_square + epsilon
    )
    grad_second = grad_first - step_first * curvature
    return kept_weights - step_first * step_dir - step_second * (mask_local * grad_second)


def call_whole(kernel, out_shape, *operands, alias={}):
    whole = pl.BlockSpec(memory_space=pltpu.VMEM)
    return pl.pallas_call(
        kernel,
        in_specs=[whole] * len(operands),
        out_specs=[whole] * len(out_shape),
        out_shape=out_shape,
        input_output_aliases=alias,
        compiler_params=pltpu.CompilerParams(vmem_limit_bytes=LIMIT),
    )(*operands)


def per_device(gram_old, activations, weights, block_mask):
    row_block, _ = gram_old.shape
    width = weights.shape[1]
    samples = activations.shape[0]
    count = lax.axis_size("row")
    if row_block % (BLK * TILES) or row_block % (16 * PARTS) or count not in (4, 8, 16) or width != BLK or samples % 16:
        return per_device_general(gram_old, activations, weights, block_mask)
    ring = Ring(count)
    row_index = lax.axis_index("row")
    col_index = lax.axis_index("col")
    per_block = row_block // BLK
    own_mask = lax.dynamic_slice(block_mask, (row_index * per_block, col_index), (per_block, 1))
    blocks = jnp.broadcast_to(own_mask.astype(jnp.float32), (per_block, width))
    panel = jax.ShapeDtypeStruct((row_block, width), jnp.float32)
    letter = jax.ShapeDtypeStruct((row_block + samples, width), jnp.bfloat16)
    eight = jax.ShapeDtypeStruct((8, width), jnp.float32)

    (message,) = call_whole(head_kernel, [letter], weights, blocks, activations)
    across = None

    def load(second):
        nonlocal across
        store, across, second = load_first(ring, gram_old, activations, second)
        return store, across, second

    own, received, store, (trace,) = ring_apply(ring, gram_old, message, activations, load)
    held = jax.ShapeDtypeStruct(store.shape, store.dtype)
    grad, message, store = call_whole(
        turn_kernel, [panel, letter, held], own, received, blocks, activations, store, alias={4: 2}
    )

    def keep(second):
        return store, across, second

    own, received, _, _ = ring_apply(ring, None, message, activations, keep)
    curve, sums = call_whole(curve_kernel, [panel, eight], trace, grad, own, received, blocks)
    sums = sum_part(sums, count)
    last = functools.partial(last_kernel, float(count * row_block))
    return call_whole(last, [panel], sums, grad, curve, weights, blocks)[0]


def solution(mesh):
    placed = (
        P(("groups", "row"), "col"),
        P("groups", "row"),
        P("row", ("groups", "col")),
        P(None, "groups"),
    )
    return jax.shard_map(
        per_device,
        mesh=mesh,
        in_specs=placed,
        out_specs=P("row", ("groups", "col")),
        check_vma=False,
    )
```

profile of v0, /device:TPU:0, one launch (start us, length us, event | category | flops | bytes accessed | tf_op | source)
XLA Modules:
  0.0 114.9 jit_solution(9966502996125429813)
XLA Ops:
  3.9 2.6 %collective-permute-start = (bf16[1920,128]{1,0:T(8,128)(2,1)S(1)}, bf16[1920,128]{1,0:T(8,128)(2,1)S(1)}, u32[]{:S(2)}, u32[]{:S(2)}) collective-permute-start(bf16[1920,128]{1,0:T(8,128)(2,1)S(1)} %shard_map.46.first), channel_id=1, source_target_pairs={{0,4},{1,2},{4,8},{5,1},{8,12},{9,5},{12,15},{13,9},{15,11},{14,13... | collective-permute-start | bytes 1474568 | tf_op jit(solution)/shard_map/ppermute | solution.py:303
  7.5 3.0 %shard_map.47 = (bf16[1792,7168]{1,0:T(8,128)(2,1)S(1)}, bf16[1792,128]{1,0:T(8,128)(2,1)S(1)}, bf16[1920,128]{1,0:T(8,128)(2,1)S(1)}) custom-call(bf16[1792,7168]{1,0:T(8,128)(2,1)} %refs_2_.3, bf16[128,1792]{1,0:T(8,128)(2,1)S(1)} %copy-done.1, bf16[1920,128]{1,0:T(8,128)(2,1)S(1)} %collective-permute-done.1.second), custom_call_target="tpu_custom_call", output_to_operand_aliasing={{2}: (2, {})} | custom-call | tf_op jit(solution)/shard_map/pallas_call | solution.py:167
  13.0 2.4 %collective-permute-start.2 = (bf16[1920,128]{1,0:T(8,128)(2,1)S(1)}, bf16[1920,128]{1,0:T(8,128)(2,1)S(1)}, u32[]{:S(2)}, u32[]{:S(2)}) collective-permute-start(bf16[1920,128]{1,0:T(8,128)(2,1)S(1)} %collective-permute-done.first), channel_id=1, source_target_pairs={{0,4},{1,2},{4,8},{5,1},{8,12},{9,5},{12,15},{13,9},{15,11},{14,13... | collective-permute-start | bytes 1474568 | tf_op jit(solution)/shard_map/ppermute | solution.py:303
  15.4 3.0 %shard_map.48 = (f32[1792,128]{1,0:T(8,128)S(1)}, f32[1792,128]{1,0:T(8,128)S(1)}, bf16[1792,7168]{1,0:T(8,128)(2,1)S(1)}, f32[8,128]{1,0:T(8,128)S(1)}) custom-call(bf16[1920,128]{1,0:T(8,128)(2,1)S(1)} %shard_map.46.first, bf16[1920,128]{1,0:T(8,128)(2,1)S(1)} %get-tuple-element.74.second, ...), custom_call_target="tpu_custom_call", output_to_operand_aliasing={{2}: (5, {})} | custom-call | flops 1644167168 | bytes 6422528 | tf_op jit(solution)/shard_map/pallas_call | solution.py:258
  21.2 2.9 %shard_map.49 = (f32[1792,128]{1,0:T(8,128)S(1)}, f32[1792,128]{1,0:T(8,128)S(1)}, bf16[1792,7168]{1,0:T(8,128)(2,1)S(1)}) custom-call(bf16[1920,128]{1,0:T(8,128)(2,1)S(1)} %collective-permute-done.first, bf16[1920,128]{1,0:T(8,128)(2,1)S(1)} %collective-permute-done.3.second, ...), custom_call_target="tpu_custom_call", output_to_operand_aliasing={{0}: (3, {}), {1}: (4, {}), {2}: (6, {})} | custom-call | flops 1644167168 | bytes 6422528 | tf_op jit(solution)/shard_map/pallas_call | solution.py:258
  24.1 2.3 %collective-permute-start.4 = (bf16[1920,128]{1,0:T(8,128)(2,1)S(1)}, bf16[1920,128]{1,0:T(8,128)(2,1)S(1)}, u32[]{:S(2)}, u32[]{:S(2)}) collective-permute-start(bf16[1920,128]{1,0:T(8,128)(2,1)S(1)} %collective-permute-done.2.first), channel_id=1, source_target_pairs={{0,4},{1,2},{4,8},{5,1},{8,12},{9,5},{12,15},{13,9},{15,11},{14,13... | collective-permute-start | bytes 1474568 | tf_op jit(solution)/shard_map/ppermute | solution.py:303
  26.5 2.9 %shard_map.50 = (f32[1792,128]{1,0:T(8,128)S(1)}, f32[1792,128]{1,0:T(8,128)S(1)}, bf16[1792,7168]{1,0:T(8,128)(2,1)S(1)}) custom-call(bf16[1920,128]{1,0:T(8,128)(2,1)S(1)} %collective-permute-done.6.first, bf16[1920,128]{1,0:T(8,128)(2,1)S(1)} %collective-permute-done.7.second, ...), custom_call_target="tpu_custom_call", output_to_operand_aliasing={{0}: (3, {}), {1}: (4, {}), {2}: (6, {})} | custom-call | flops 493250144 | bytes 1926758 | tf_op jit(solution)/shard_map/pallas_call | solution.py:258
  29.4 2.3 %collective-permute-start.10 = (bf16[1920,128]{1,0:T(8,128)(2,1)S(1)}, bf16[1920,128]{1,0:T(8,128)(2,1)S(1)}, u32[]{:S(2)}, u32[]{:S(2)}) collective-permute-start(bf16[1920,128]{1,0:T(8,128)(2,1)S(1)} %collective-permute-done.5.second), channel_id=1, source_target_pairs={{0,4},{1,2},{4,8},{5,1},{8,12},{9,5},{12,15},{13,9},{15,11},{14,13... | collective-permute-start | bytes 1474568 | tf_op jit(solution)/shard_map/ppermute | solution.py:306
  34.6 2.4 %collective-permute-start.8 = (bf16[1920,128]{1,0:T(8,128)(2,1)S(1)}, bf16[1920,128]{1,0:T(8,128)(2,1)S(1)}, u32[]{:S(2)}, u32[]{:S(2)}) collective-permute-start(bf16[1920,128]{1,0:T(8,128)(2,1)S(1)} %collective-permute-done.4.first), channel_id=1, source_target_pairs={{0,4},{1,2},{4,8},{5,1},{8,12},{9,5},{12,15},{13,9},{15,11},{14,13... | collective-permute-start | bytes 1474568 | tf_op jit(solution)/shard_map/ppermute | solution.py:313
  37.0 2.9 %collective-permute-done.10.second = bf16[1920,128]{1,0:T(8,128)(2,1)S(1)} collective-permute-done((bf16[1920,128]{1,0:T(8,128)(2,1)S(1)}, bf16[1920,128]{1,0:T(8,128)(2,1)S(1)}, u32[]{:S(2)}, u32[]{:S(2)}) %collective-permute-start.10) | collective-permute-done | bytes 491552 | tf_op jit(solution)/shard_map/ppermute | solution.py:306
  41.8 3.4 %collective-permute-done.8.first = bf16[1920,128]{1,0:T(8,128)(2,1)S(1)} collective-permute-done((bf16[1920,128]{1,0:T(8,128)(2,1)S(1)}, bf16[1920,128]{1,0:T(8,128)(2,1)S(1)}, u32[]{:S(2)}, u32[]{:S(2)}) %collective-permute-start.8) | collective-permute-done | bytes 491552 | tf_op jit(solution)/shard_map/ppermute | solution.py:313
  47.0 2.3 %collective-permute-start.13 = (f32[1792,128]{1,0:T(8,128)S(1)}, f32[1792,128]{1,0:T(8,128)S(1)}, u32[]{:S(2)}, u32[]{:S(2)}) collective-permute-start(f32[1792,128]{1,0:T(8,128)S(1)} %get-tuple-element.105), channel_id=1, source_target_pairs={{0,1},{1,0},{2,3},{3,2},{4,5},{5,4},{6,7},{7,6},{8,9},{9,8},{10,11... | collective-permute-start | bytes 2752520 | tf_op jit(solution)/shard_map/ppermute | solution.py:22
  56.3 4.7 %collective-permute-done.14.first = bf16[1920,128]{1,0:T(8,128)(2,1)S(1)} collective-permute-done((bf16[1920,128]{1,0:T(8,128)(2,1)S(1)}, bf16[1920,128]{1,0:T(8,128)(2,1)S(1)}, u32[]{:S(2)}, u32[]{:S(2)}) %collective-permute-start.14) | collective-permute-done | bytes 491552 | tf_op jit(solution)/shard_map/ppermute | solution.py:303
  61.0 2.5 %collective-permute-start.15 = (bf16[1920,128]{1,0:T(8,128)(2,1)S(1)}, bf16[1920,128]{1,0:T(8,128)(2,1)S(1)}, u32[]{:S(2)}, u32[]{:S(2)}) collective-permute-start(bf16[1920,128]{1,0:T(8,128)(2,1)S(1)} %collective-permute-done.14.first), channel_id=1, source_target_pairs={{0,4},{1,2},{4,8},{5,1},{8,12},{9,5},{12,15},{13,9},{15,11},{14,13... | collective-permute-start | bytes 1474568 | tf_op jit(solution)/shard_map/ppermute | solution.py:303
  66.3 2.4 %collective-permute-start.19 = (bf16[1920,128]{1,0:T(8,128)(2,1)S(1)}, bf16[1920,128]{1,0:T(8,128)(2,1)S(1)}, u32[]{:S(2)}, u32[]{:S(2)}) collective-permute-start(bf16[1920,128]{1,0:T(8,128)(2,1)S(1)} %collective-permute-done.17.second), channel_id=1, source_target_pairs={{0,4},{1,2},{4,8},{5,1},{8,12},{9,5},{12,15},{13,9},{15,11},{14,13... | collective-permute-start | bytes 1474568 | tf_op jit(solution)/shard_map/ppermute | solution.py:306
  71.5 2.5 %collective-permute-start.18 = (bf16[1920,128]{1,0:T(8,128)(2,1)S(1)}, bf16[1920,128]{1,0:T(8,128)(2,1)S(1)}, u32[]{:S(2)}, u32[]{:S(2)}) collective-permute-start(bf16[1920,128]{1,0:T(8,128)(2,1)S(1)} %collective-permute-done.15.first), channel_id=1, source_target_pairs={{0,4},{1,2},{4,8},{5,1},{8,12},{9,5},{12,15},{13,9},{15,11},{14,13... | collective-permute-start | bytes 1474568 | tf_op jit(solution)/shard_map/ppermute | solution.py:303
  76.8 2.5 %collective-permute-start.24 = (bf16[1920,128]{1,0:T(8,128)(2,1)S(1)}, bf16[1920,128]{1,0:T(8,128)(2,1)S(1)}, u32[]{:S(2)}, u32[]{:S(2)}) collective-permute-start(bf16[1920,128]{1,0:T(8,128)(2,1)S(1)} %collective-permute-done.19.second), channel_id=1, source_target_pairs={{0,4},{1,2},{4,8},{5,1},{8,12},{9,5},{12,15},{13,9},{15,11},{14,13... | collective-permute-start | bytes 1474568 | tf_op jit(solution)/shard_map/ppermute | solution.py:306
  82.1 2.5 %collective-permute-start.22 = (bf16[1920,128]{1,0:T(8,128)(2,1)S(1)}, bf16[1920,128]{1,0:T(8,128)(2,1)S(1)}, u32[]{:S(2)}, u32[]{:S(2)}) collective-permute-start(bf16[1920,128]{1,0:T(8,128)(2,1)S(1)} %collective-permute-done.18.first), channel_id=1, source_target_pairs={{0,4},{1,2},{4,8},{5,1},{8,12},{9,5},{12,15},{13,9},{15,11},{14,13... | collective-permute-start | bytes 1474568 | tf_op jit(solution)/shard_map/ppermute | solution.py:313
  84.5 2.8 %collective-permute-done.24.second = bf16[1920,128]{1,0:T(8,128)(2,1)S(1)} collective-permute-done((bf16[1920,128]{1,0:T(8,128)(2,1)S(1)}, bf16[1920,128]{1,0:T(8,128)(2,1)S(1)}, u32[]{:S(2)}, u32[]{:S(2)}) %collective-permute-start.24) | collective-permute-done | bytes 491552 | tf_op jit(solution)/shard_map/ppermute | solution.py:306
  89.2 3.4 %collective-permute-done.22.first = bf16[1920,128]{1,0:T(8,128)(2,1)S(1)} collective-permute-done((bf16[1920,128]{1,0:T(8,128)(2,1)S(1)}, bf16[1920,128]{1,0:T(8,128)(2,1)S(1)}, u32[]{:S(2)}, u32[]{:S(2)}) %collective-permute-start.22) | collective-permute-done | bytes 491552 | tf_op jit(solution)/shard_map/ppermute | solution.py:313
  94.4 2.3 %collective-permute-start.27 = (f32[1792,128]{1,0:T(8,128)S(1)}, f32[1792,128]{1,0:T(8,128)S(1)}, u32[]{:S(2)}, u32[]{:S(2)}) collective-permute-start(f32[1792,128]{1,0:T(8,128)S(1)} %get-tuple-element.138), channel_id=1, source_target_pairs={{0,1},{1,0},{2,3},{3,2},{4,5},{5,4},{6,7},{7,6},{8,9},{9,8},{10,11... | collective-permute-start | bytes 2752520 | tf_op jit(solution)/shard_map/ppermute | solution.py:22
  102.0 2.5 %collective-permute-start.30 = (f32[8,128]{1,0:T(8,128)S(1)}, f32[8,128]{1,0:T(8,128)S(1)}, u32[]{:S(2)}, u32[]{:S(2)}) collective-permute-start(f32[8,128]{1,0:T(8,128)S(1)} %add.23), channel_id=1, source_target_pairs={{0,4},{1,5},{2,6},{3,7},{4,0},{5,1},{6,2},{7,3},{8,12},{9,13},{10,... | collective-permute-start | bytes 12296 | tf_op jit(solution)/shard_map/ppermute | solution.py:31
  106.1 2.9 %collective-permute-done.31 = f32[8,128]{1,0:T(8,128)S(1)} collective-permute-done((f32[8,128]{1,0:T(8,128)S(1)}, f32[8,128]{1,0:T(8,128)S(1)}, u32[]{:S(2)}, u32[]{:S(2)}) %collective-permute-start.31) | collective-permute-done | bytes 4128 | tf_op jit(solution)/shard_map/ppermute | solution.py:31
  109.0 2.8 %collective-permute-start.32 = (f32[8,128]{1,0:T(8,128)S(1)}, f32[8,128]{1,0:T(8,128)S(1)}, u32[]{:S(2)}, u32[]{:S(2)}) collective-permute-start(f32[8,128]{1,0:T(8,128)S(1)} %add_add_fusion), channel_id=1, source_target_pairs={{0,8},{1,9},{2,10},{3,11},{4,12},{5,13},{6,14},{7,15},{8,0},{9,1},... | collective-permute-start | bytes 12296 | tf_op jit(solution)/shard_map/ppermute | solution.py:31
  (76 shorter events, 48.5 us)
Async XLA Ops:
  3.9 9.1 %collective-permute-start = (bf16[1920,128]{1,0:T(8,128)(2,1)S(1)}, bf16[1920,128]{1,0:T(8,128)(2,1)S(1)}, u32[]{:S(2)}, u32[]{:S(2)}) collective-permute-start(bf16[1920,128]{1,0:T(8,128)(2,1)S(1)} %shard_map.46.first), channel_id=1, source_target_pairs={{0,4},{1,2},{4,8},{5,1},{8,12},{9,5},{12,15},{13,9},{15,11},{14,13... | collective-permute-start | bytes 1474568 | tf_op jit(solution)/shard_map/ppermute | solution.py:303
  10.5 8.3 %collective-permute-start.3 = (bf16[1920,128]{1,0:T(8,128)(2,1)S(1)}, bf16[1920,128]{1,0:T(8,128)(2,1)S(1)}, u32[]{:S(2)}, u32[]{:S(2)}) collective-permute-start(bf16[1920,128]{1,0:T(8,128)(2,1)S(1)} %get-tuple-element.74.second), channel_id=1, source_target_pairs={{0,4},{1,2},{4,8},{5,1},{8,12},{9,5},{12,15},{13,9},{15,11},{14,13... | collective-permute-start | bytes 1474568 | tf_op jit(solution)/shard_map/ppermute | solution.py:306
  13.0 11.1 %collective-permute-start.2 = (bf16[1920,128]{1,0:T(8,128)(2,1)S(1)}, bf16[1920,128]{1,0:T(8,128)(2,1)S(1)}, u32[]{:S(2)}, u32[]{:S(2)}) collective-permute-start(bf16[1920,128]{1,0:T(8,128)(2,1)S(1)} %collective-permute-done.first), channel_id=1, source_target_pairs={{0,4},{1,2},{4,8},{5,1},{8,12},{9,5},{12,15},{13,9},{15,11},{14,13... | collective-permute-start | bytes 1474568 | tf_op jit(solution)/shard_map/ppermute | solution.py:303
  18.4 5.7 %collective-permute-start.6 = (bf16[1920,128]{1,0:T(8,128)(2,1)S(1)}, bf16[1920,128]{1,0:T(8,128)(2,1)S(1)}, u32[]{:S(2)}, u32[]{:S(2)}) collective-permute-start(bf16[1920,128]{1,0:T(8,128)(2,1)S(1)} %collective-permute-done.first), channel_id=1, source_target_pairs={{0,1},{1,0},{2,3},{3,2},{4,5},{5,4},{6,7},{7,6},{8,9},{9,8},{10,11... | collective-permute-start | bytes 1474568 | tf_op jit(solution)/shard_map/ppermute | solution.py:22
  18.8 7.6 %collective-permute-start.7 = (bf16[1920,128]{1,0:T(8,128)(2,1)S(1)}, bf16[1920,128]{1,0:T(8,128)(2,1)S(1)}, u32[]{:S(2)}, u32[]{:S(2)}) collective-permute-start(bf16[1920,128]{1,0:T(8,128)(2,1)S(1)} %collective-permute-done.3.second), channel_id=1, source_target_pairs={{0,1},{1,0},{2,3},{3,2},{4,5},{5,4},{6,7},{7,6},{8,9},{9,8},{10,11... | collective-permute-start | bytes 1474568 | tf_op jit(solution)/shard_map/ppermute | solution.py:22
  19.0 10.4 %collective-permute-start.5 = (bf16[1920,128]{1,0:T(8,128)(2,1)S(1)}, bf16[1920,128]{1,0:T(8,128)(2,1)S(1)}, u32[]{:S(2)}, u32[]{:S(2)}) collective-permute-start(bf16[1920,128]{1,0:T(8,128)(2,1)S(1)} %collective-permute-done.3.second), channel_id=1, source_target_pairs={{0,4},{1,2},{4,8},{5,1},{8,12},{9,5},{12,15},{13,9},{15,11},{14,13... | collective-permute-start | bytes 1474568 | tf_op jit(solution)/shard_map/ppermute | solution.py:306
  24.1 10.5 %collective-permute-start.4 = (bf16[1920,128]{1,0:T(8,128)(2,1)S(1)}, bf16[1920,128]{1,0:T(8,128)(2,1)S(1)}, u32[]{:S(2)}, u32[]{:S(2)}) collective-permute-start(bf16[1920,128]{1,0:T(8,128)(2,1)S(1)} %collective-permute-done.2.first), channel_id=1, source_target_pairs={{0,4},{1,2},{4,8},{5,1},{8,12},{9,5},{12,15},{13,9},{15,11},{14,13... | collective-permute-start | bytes 1474568 | tf_op jit(solution)/shard_map/ppermute | solution.py:303
  29.4 10.5 %collective-permute-start.10 = (bf16[1920,128]{1,0:T(8,128)(2,1)S(1)}, bf16[1920,128]{1,0:T(8,128)(2,1)S(1)}, u32[]{:S(2)}, u32[]{:S(2)}) collective-permute-start(bf16[1920,128]{1,0:T(8,128)(2,1)S(1)} %collective-permute-done.5.second), channel_id=1, source_target_pairs={{0,4},{1,2},{4,8},{5,1},{8,12},{9,5},{12,15},{13,9},{15,11},{14,13... | collective-permute-start | bytes 1474568 | tf_op jit(solution)/shard_map/ppermute | solution.py:306
  34.6 5.3 %collective-permute-start.9 = (bf16[1920,128]{1,0:T(8,128)(2,1)S(1)}, bf16[1920,128]{1,0:T(8,128)(2,1)S(1)}, u32[]{:S(2)}, u32[]{:S(2)}) collective-permute-start(bf16[1920,128]{1,0:T(8,128)(2,1)S(1)} %collective-permute-done.4.first), channel_id=1, source_target_pairs={{0,1},{1,0},{2,3},{3,2},{4,5},{5,4},{6,7},{7,6},{8,9},{9,8},{10,11... | collective-permute-start | bytes 1474568 | tf_op jit(solution)/shard_map/ppermute | solution.py:22
  34.6 10.5 %collective-permute-start.8 = (bf16[1920,128]{1,0:T(8,128)(2,1)S(1)}, bf16[1920,128]{1,0:T(8,128)(2,1)S(1)}, u32[]{:S(2)}, u32[]{:S(2)}) collective-permute-start(bf16[1920,128]{1,0:T(8,128)(2,1)S(1)} %collective-permute-done.4.first), channel_id=1, source_target_pairs={{0,4},{1,2},{4,8},{5,1},{8,12},{9,5},{12,15},{13,9},{15,11},{14,13... | collective-permute-start | bytes 1474568 | tf_op jit(solution)/shard_map/ppermute | solution.py:313
  47.0 4.4 %collective-permute-start.13 = (f32[1792,128]{1,0:T(8,128)S(1)}, f32[1792,128]{1,0:T(8,128)S(1)}, u32[]{:S(2)}, u32[]{:S(2)}) collective-permute-start(f32[1792,128]{1,0:T(8,128)S(1)} %get-tuple-element.105), channel_id=1, source_target_pairs={{0,1},{1,0},{2,3},{3,2},{4,5},{5,4},{6,7},{7,6},{8,9},{9,8},{10,11... | collective-permute-start | bytes 2752520 | tf_op jit(solution)/shard_map/ppermute | solution.py:22
  52.3 8.7 %collective-permute-start.14 = (bf16[1920,128]{1,0:T(8,128)(2,1)S(1)}, bf16[1920,128]{1,0:T(8,128)(2,1)S(1)}, u32[]{:S(2)}, u32[]{:S(2)}) collective-permute-start(bf16[1920,128]{1,0:T(8,128)(2,1)S(1)} %get-tuple-element.109.first), channel_id=1, source_target_pairs={{0,4},{1,2},{4,8},{5,1},{8,12},{9,5},{12,15},{13,9},{15,11},{14,13... | collective-permute-start | bytes 1474568 | tf_op jit(solution)/shard_map/ppermute | solution.py:303
  54.6 11.6 %collective-permute-start.17 = (bf16[1920,128]{1,0:T(8,128)(2,1)S(1)}, bf16[1920,128]{1,0:T(8,128)(2,1)S(1)}, u32[]{:S(2)}, u32[]{:S(2)}) collective-permute-start(bf16[1920,128]{1,0:T(8,128)(2,1)S(1)} %collective-permute-done.16.second), channel_id=1, source_target_pairs={{0,4},{1,2},{4,8},{5,1},{8,12},{9,5},{12,15},{13,9},{15,11},{14,13... | collective-permute-start | bytes 1474568 | tf_op jit(solution)/shard_map/ppermute | solution.py:306
  61.0 10.5 %collective-permute-start.15 = (bf16[1920,128]{1,0:T(8,128)(2,1)S(1)}, bf16[1920,128]{1,0:T(8,128)(2,1)S(1)}, u32[]{:S(2)}, u32[]{:S(2)}) collective-permute-start(bf16[1920,128]{1,0:T(8,128)(2,1)S(1)} %collective-permute-done.14.first), channel_id=1, source_target_pairs={{0,4},{1,2},{4,8},{5,1},{8,12},{9,5},{12,15},{13,9},{15,11},{14,13... | collective-permute-start | bytes 1474568 | tf_op jit(solution)/shard_map/ppermute | solution.py:303
  65.7 8.3 %collective-permute-start.20 = (bf16[1920,128]{1,0:T(8,128)(2,1)S(1)}, bf16[1920,128]{1,0:T(8,128)(2,1)S(1)}, u32[]{:S(2)}, u32[]{:S(2)}) collective-permute-start(bf16[1920,128]{1,0:T(8,128)(2,1)S(1)} %collective-permute-done.14.first), channel_id=1, source_target_pairs={{0,1},{1,0},{2,3},{3,2},{4,5},{5,4},{6,7},{7,6},{8,9},{9,8},{10,11... | collective-permute-start | bytes 1474568 | tf_op jit(solution)/shard_map/ppermute | solution.py:22
  66.2 7.8 %collective-permute-start.21 = (bf16[1920,128]{1,0:T(8,128)(2,1)S(1)}, bf16[1920,128]{1,0:T(8,128)(2,1)S(1)}, u32[]{:S(2)}, u32[]{:S(2)}) collective-permute-start(bf16[1920,128]{1,0:T(8,128)(2,1)S(1)} %collective-permute-done.17.second), channel_id=1, source_target_pairs={{0,1},{1,0},{2,3},{3,2},{4,5},{5,4},{6,7},{7,6},{8,9},{9,8},{10,11... | collective-permute-start | bytes 1474568 | tf_op jit(solution)/shard_map/ppermute | solution.py:22
  66.3 10.5 %collective-permute-start.19 = (bf16[1920,128]{1,0:T(8,128)(2,1)S(1)}, bf16[1920,128]{1,0:T(8,128)(2,1)S(1)}, u32[]{:S(2)}, u32[]{:S(2)}) collective-permute-start(bf16[1920,128]{1,0:T(8,128)(2,1)S(1)} %collective-permute-done.17.second), channel_id=1, source_target_pairs={{0,4},{1,2},{4,8},{5,1},{8,12},{9,5},{12,15},{13,9},{15,11},{14,13... | collective-permute-start | bytes 1474568 | tf_op jit(solution)/shard_map/ppermute | solution.py:306
  71.5 10.5 %collective-permute-start.18 = (bf16[1920,128]{1,0:T(8,128)(2,1)S(1)}, bf16[1920,128]{1,0:T(8,128)(2,1)S(1)}, u32[]{:S(2)}, u32[]{:S(2)}) collective-permute-start(bf16[1920,128]{1,0:T(8,128)(2,1)S(1)} %collective-permute-done.15.first), channel_id=1, source_target_pairs={{0,4},{1,2},{4,8},{5,1},{8,12},{9,5},{12,15},{13,9},{15,11},{14,13... | collective-permute-start | bytes 1474568 | tf_op jit(solution)/shard_map/ppermute | solution.py:303
  76.8 10.5 %collective-permute-start.24 = (bf16[1920,128]{1,0:T(8,128)(2,1)S(1)}, bf16[1920,128]{1,0:T(8,128)(2,1)S(1)}, u32[]{:S(2)}, u32[]{:S(2)}) collective-permute-start(bf16[1920,128]{1,0:T(8,128)(2,1)S(1)} %collective-permute-done.19.second), channel_id=1, source_target_pairs={{0,4},{1,2},{4,8},{5,1},{8,12},{9,5},{12,15},{13,9},{15,11},{14,13... | collective-permute-start | bytes 1474568 | tf_op jit(solution)/shard_map/ppermute | solution.py:306
  82.0 5.3 %collective-permute-start.23 = (bf16[1920,128]{1,0:T(8,128)(2,1)S(1)}, bf16[1920,128]{1,0:T(8,128)(2,1)S(1)}, u32[]{:S(2)}, u32[]{:S(2)}) collective-permute-start(bf16[1920,128]{1,0:T(8,128)(2,1)S(1)} %collective-permute-done.18.first), channel_id=1, source_target_pairs={{0,1},{1,0},{2,3},{3,2},{4,5},{5,4},{6,7},{7,6},{8,9},{9,8},{10,11... | collective-permute-start | bytes 1474568 | tf_op jit(solution)/shard_map/ppermute | solution.py:22
  82.1 10.5 %collective-permute-start.22 = (bf16[1920,128]{1,0:T(8,128)(2,1)S(1)}, bf16[1920,128]{1,0:T(8,128)(2,1)S(1)}, u32[]{:S(2)}, u32[]{:S(2)}) collective-permute-start(bf16[1920,128]{1,0:T(8,128)(2,1)S(1)} %collective-permute-done.18.first), channel_id=1, source_target_pairs={{0,4},{1,2},{4,8},{5,1},{8,12},{9,5},{12,15},{13,9},{15,11},{14,13... | collective-permute-start | bytes 1474568 | tf_op jit(solution)/shard_map/ppermute | solution.py:313
  94.4 4.4 %collective-permute-start.27 = (f32[1792,128]{1,0:T(8,128)S(1)}, f32[1792,128]{1,0:T(8,128)S(1)}, u32[]{:S(2)}, u32[]{:S(2)}) collective-permute-start(f32[1792,128]{1,0:T(8,128)S(1)} %get-tuple-element.138), channel_id=1, source_target_pairs={{0,1},{1,0},{2,3},{3,2},{4,5},{5,4},{6,7},{7,6},{8,9},{9,8},{10,11... | collective-permute-start | bytes 2752520 | tf_op jit(solution)/shard_map/ppermute | solution.py:22
  104.5 4.5 %collective-permute-start.31 = (f32[8,128]{1,0:T(8,128)S(1)}, f32[8,128]{1,0:T(8,128)S(1)}, u32[]{:S(2)}, u32[]{:S(2)}) collective-permute-start(f32[8,128]{1,0:T(8,128)S(1)} %add.23), channel_id=1, source_target_pairs={{0,6},{1,7},{2,4},{3,5},{4,2},{5,3},{6,0},{7,1},{8,14},{9,15},{10,... | collective-permute-start | bytes 12296 | tf_op jit(solution)/shard_map/ppermute | solution.py:31
  109.0 4.5 %collective-permute-start.32 = (f32[8,128]{1,0:T(8,128)S(1)}, f32[8,128]{1,0:T(8,128)S(1)}, u32[]{:S(2)}, u32[]{:S(2)}) collective-permute-start(f32[8,128]{1,0:T(8,128)S(1)} %add_add_fusion), channel_id=1, source_target_pairs={{0,8},{1,9},{2,10},{3,11},{4,12},{5,13},{6,14},{7,15},{8,0},{9,1},... | collective-permute-start | bytes 12296 | tf_op jit(solution)/shard_map/ppermute | solution.py:31
  (14 other events, 60.1 us)
where the time goes:
time: 115 us
  starting transfers between devices  45.7 us (40%)
  waiting for transfers between devices  40 us (35%)
  Pallas kernels  25 us (22%)
  local copies, waits for them, and re-layouts  3.3 us (3%)
    pallas_call x14, Pallas kernels, product(): pl.pallas_call(functools.partial(product_kernel, ring, slot, loads, with_...  19.6 us
    ppermute x6, starting transfers between devices, ring_apply(): came = lax.ppermute(after(first, acc[:1]), AXES, ring.shift())  14.6 us
    ppermute x6, starting transfers between devices, ring_apply(): second = lax.ppermute(after(second, acc[:1]), AXES, ring.shift())  12.9 us
    ppermute x14, waiting for transfers between devices, swap(): lax.ppermute(value, axis, [(i, i ^ distance) for i in range(lax.axis_size...  11.6 us
    ppermute x6, waiting for transfers between devices, ring_apply(): came = lax.ppermute(after(first, acc[:1]), AXES, ring.shift())  7.45 us
    ppermute x5, starting transfers between devices, sum_part(): value += sum((lax.ppermute(value, AXES, pairs) for pairs in swaps))  7.27 us
    ppermute x6, waiting for transfers between devices, ring_apply(): second = lax.ppermute(after(second, acc[:1]), AXES, ring.shift())  7.12 us
    ppermute x5, waiting for transfers between devices, sum_part(): value += sum((lax.ppermute(value, AXES, pairs) for pairs in swaps))  7.03 us
  transfers between devices with their start and end apart: 33, of which 22 were waited for; matrix products, arithmetic and copies ran while one was open for 0% of the time, Pallas kernels for 20%

commit v1 on v0

--- a/solution.py
+++ b/solution.py
@@ -11,6 +11,7 @@
 TILES = 1
 PARTS = 4
 LIMIT = 8 * 1024 * 1024
+HEAD_LIMIT = 60 * 1024 * 1024
 AXES = ("row", "col")
 WEIGHTS = ((1, 1, 0.3, 0.3, 8, 0.02, 0.02), (1, 0.02, 0.3, 2, 4, 0.3, 4))
 
@@ -325,13 +326,40 @@
     ).astype(message.dtype)
 
 
-def head_kernel(weights, blocks, acts, message):
+def head_kernel(mask, weights, acts, message, kept, dense, samples, sems):
+    copies = [
+        pltpu.make_async_copy(mask, kept, sems.at[0]),
+        pltpu.make_async_copy(weights, dense, sems.at[1]),
+        pltpu.make_async_copy(acts, samples, sems.at[2]),
+    ]
+    for copy in copies:
+        copy.start()
+    for copy in copies:
+        copy.wait()
     rows = weights.shape[0]
+    top, column = lax.axis_index("row") * (rows // BLK), lax.axis_index("col")
     for block in range(rows // BLK):
         here = slice(block * BLK, (block + 1) * BLK)
-        dense = weights[here, :]
-        message[here, :] = (blocks[block : block + 1, :] * dense - dense).astype(message.dtype)
-    put_message(message, acts, rows)
+        factor = kept[column, top + block].astype(jnp.float32)
+        message[here, :] = (factor * dense[here, :] - dense[here, :]).astype(message.dtype)
+    put_message(message, samples, rows)
+
+
+def first_message(block_mask, weights, acts, letter):
+    mask = block_mask.T
+    return pl.pallas_call(
+        head_kernel,
+        in_specs=[pl.BlockSpec(memory_space=pltpu.HBM)] * 3,
+        out_specs=pl.BlockSpec(memory_space=pltpu.VMEM),
+        out_shape=letter,
+        scratch_shapes=[
+            pltpu.SMEM(mask.shape, mask.dtype),
+            pltpu.VMEM(weights.shape, weights.dtype),
+            pltpu.VMEM(acts.shape, acts.dtype),
+            pltpu.SemaphoreType.DMA((3,)),
+        ],
+        compiler_params=pltpu.CompilerParams(vmem_limit_bytes=HEAD_LIMIT),
+    )(mask, weights, acts)
 
 
 def turn_kernel(own, received, blocks, acts, _, grad, message, __):
@@ -473,7 +501,7 @@
     letter = jax.ShapeDtypeStruct((row_block + samples, width), jnp.bfloat16)
     eight = jax.ShapeDtypeStruct((8, width), jnp.float32)
 
-    (message,) = call_whole(head_kernel, [letter], weights, blocks, activations)
+    message = first_message(block_mask, weights, activations, letter)
     across = None
 
     def load(second):

time: 115 us -> 147 us (1.28)
  local copies, waits for them, and re-layouts: 3.3 us -> 34.7 us
  starting transfers between devices: 45.7 us -> 40.3 us
  Pallas kernels: 25 us -> 28.3 us
  waiting for transfers between devices: 40 us -> 42.9 us
    unnamed x10 -> x18, local copies, waits for them, and re-layouts: 3.22 us -> 34.7 us
    pallas_call x0 -> x1, Pallas kernels: none -> 2.43 us  [first_message(): pl.pallas_call(head_kernel, in_specs=[pl.BlockSpec(memory_space=pltpu.HBM...]
    ppermute x5, starting transfers between devices: 7.27 us -> 4.91 us  [sum_part(): value += sum((lax.ppermute(value, AXES, pairs) for pairs in swaps))]
    ppermute x6, starting transfers between devices: 14.6 us -> 12.4 us  [ring_apply(): came = lax.ppermute(after(first, acc[:1]), AXES, ring.shift())]
    ppermute x5, waiting for transfers between devices: 7.03 us -> 9.01 us  [sum_part(): value += sum((lax.ppermute(value, AXES, pairs) for pairs in swaps))]
    pallas_call x4 -> x3, Pallas kernels: 2.42 us -> 3.28 us  [call_whole(): pl.pallas_call(kernel, in_specs=[whole] * len(operands), out_specs=[whole...]
  transfers between devices with their start and end apart: 33 -> 33, of which waited for: 22 -> 20; matrix products, arithmetic and copies ran while one was open for 0% -> 0% of each run, Pallas kernels for 20% -> 15%
where the time goes in v1:
time: 147 us
  waiting for transfers between devices  42.9 us (29%)
  starting transfers between devices  40.3 us (27%)
  local copies, waits for them, and re-layouts  34.7 us (24%)
  Pallas kernels  28.3 us (19%)
    unnamed x18, local copies, waits for them, and re-layouts  34.7 us
    pallas_call x14, Pallas kernels, product(): pl.pallas_call(functools.partial(product_kernel, ring, slot, loads, with_...  19.6 us
    ppermute x6, starting transfers between devices, ring_apply(): came = lax.ppermute(after(first, acc[:1]), AXES, ring.shift())  12.4 us
    ppermute x6, starting transfers between devices, ring_apply(): second = lax.ppermute(after(second, acc[:1]), AXES, ring.shift())  12 us
    ppermute x14, waiting for transfers between devices, swap(): lax.ppermute(value, axis, [(i, i ^ distance) for i in range(lax.axis_size...  11.7 us
    ppermute x5, waiting for transfers between devices, sum_part(): value += sum((lax.ppermute(value, AXES, pairs) for pairs in swaps))  9.01 us
    ppermute x6, waiting for transfers between devices, ring_apply(): second = lax.ppermute(after(second, acc[:1]), AXES, ring.shift())  8.49 us
    ppermute x6, waiting for transfers between devices, ring_apply(): came = lax.ppermute(after(first, acc[:1]), AXES, ring.shift())  6.98 us
  transfers between devices with their start and end apart: 33, of which 20 were waited for; matrix products, arithmetic and copies ran while one was open for 0% of the time, Pallas kernels for 15%

profile of v1, /device:TPU:0, one launch (start us, length us, event | category | flops | bytes accessed | tf_op | source)
XLA Modules:
  0.0 146.6 jit_solution(12761838015585983429)
XLA Ops:
  0.0 2.4 %shard_map.46.first = bf16[1920,128]{1,0:T(8,128)(2,1)} custom-call(s32[2,112]{1,0:T(2,128)} %bitcast.3, f32[1792,128]{1,0:T(8,128)} %weights.3, bf16[128,1792]{1,0:T(8,128)(2,1)} %acts.5), custom_call_target="tpu_custom_call" | custom-call | tf_op jit(solution)/shard_map/pallas_call | solution.py:350
  3.0 2.6 %collective-permute-start = (bf16[1920,128]{1,0:T(8,128)(2,1)}, bf16[1920,128]{1,0:T(8,128)(2,1)S(1)}, u32[]{:S(2)}, u32[]{:S(2)}) collective-permute-start(bf16[1920,128]{1,0:T(8,128)(2,1)} %shard_map.46.first), channel_id=1, source_target_pairs={{0,4},{1,2},{4,8},{5,1},{8,12},{9,5},{12,15},{13,9},{15,11},{14,13... | collective-permute-start | bytes 1474568 | tf_op jit(solution)/shard_map/ppermute | solution.py:304
  6.6 3.0 %shard_map.47 = (bf16[1792,7168]{1,0:T(8,128)(2,1)S(1)}, bf16[1792,128]{1,0:T(8,128)(2,1)S(1)}, bf16[1920,128]{1,0:T(8,128)(2,1)S(1)}) custom-call(bf16[1792,7168]{1,0:T(8,128)(2,1)} %refs_2_.3, bf16[128,1792]{1,0:T(8,128)(2,1)S(1)} %copy-done.4, bf16[1920,128]{1,0:T(8,128)(2,1)S(1)} %collective-permute-done.1.second), custom_call_target="tpu_custom_call", output_to_operand_aliasing={{2}: (2, {})} | custom-call | tf_op jit(solution)/shard_map/pallas_call | solution.py:168
  12.3 2.4 %collective-permute-start.2 = (bf16[1920,128]{1,0:T(8,128)(2,1)S(1)}, bf16[1920,128]{1,0:T(8,128)(2,1)S(1)}, u32[]{:S(2)}, u32[]{:S(2)}) collective-permute-start(bf16[1920,128]{1,0:T(8,128)(2,1)S(1)} %collective-permute-done.first), channel_id=1, source_target_pairs={{0,4},{1,2},{4,8},{5,1},{8,12},{9,5},{12,15},{13,9},{15,11},{14,13... | collective-permute-start | bytes 1474568 | tf_op jit(solution)/shard_map/ppermute | solution.py:304
  14.6 3.0 %shard_map.48 = (f32[1792,128]{1,0:T(8,128)S(1)}, f32[1792,128]{1,0:T(8,128)S(1)}, bf16[1792,7168]{1,0:T(8,128)(2,1)S(1)}, f32[8,128]{1,0:T(8,128)S(1)}) custom-call(bf16[1920,128]{1,0:T(8,128)(2,1)S(1)} %copy-done.7, bf16[1920,128]{1,0:T(8,128)(2,1)S(1)} %get-tuple-element.74.second, ...), custom_call_target="tpu_custom_call", output_to_operand_aliasing={{2}: (5, {})} | custom-call | flops 1644167168 | bytes 6422528 | tf_op jit(solution)/shard_map/pallas_call | solution.py:259
  20.5 2.9 %shard_map.49 = (f32[1792,128]{1,0:T(8,128)S(1)}, f32[1792,128]{1,0:T(8,128)S(1)}, bf16[1792,7168]{1,0:T(8,128)(2,1)S(1)}) custom-call(bf16[1920,128]{1,0:T(8,128)(2,1)S(1)} %collective-permute-done.first, bf16[1920,128]{1,0:T(8,128)(2,1)S(1)} %collective-permute-done.3.second, ...), custom_call_target="tpu_custom_call", output_to_operand_aliasing={{0}: (3, {}), {1}: (4, {}), {2}: (6, {})} | custom-call | flops 1644167168 | bytes 6422528 | tf_op jit(solution)/shard_map/pallas_call | solution.py:259
  25.8 2.9 %shard_map.50 = (f32[1792,128]{1,0:T(8,128)S(1)}, f32[1792,128]{1,0:T(8,128)S(1)}, bf16[1792,7168]{1,0:T(8,128)(2,1)S(1)}) custom-call(bf16[1920,128]{1,0:T(8,128)(2,1)S(1)} %collective-permute-done.6.first, bf16[1920,128]{1,0:T(8,128)(2,1)S(1)} %collective-permute-done.7.second, ...), custom_call_target="tpu_custom_call", output_to_operand_aliasing={{0}: (3, {}), {1}: (4, {}), {2}: (6, {})} | custom-call | flops 493250144 | bytes 1926758 | tf_op jit(solution)/shard_map/pallas_call | solution.py:259
  28.7 2.3 %collective-permute-start.10 = (bf16[1920,128]{1,0:T(8,128)(2,1)S(1)}, bf16[1920,128]{1,0:T(8,128)(2,1)S(1)}, u32[]{:S(2)}, u32[]{:S(2)}) collective-permute-start(bf16[1920,128]{1,0:T(8,128)(2,1)S(1)} %collective-permute-done.5.second), channel_id=1, source_target_pairs={{0,4},{1,2},{4,8},{5,1},{8,12},{9,5},{12,15},{13,9},{15,11},{14,13... | collective-permute-start | bytes 1474568 | tf_op jit(solution)/shard_map/ppermute | solution.py:307
  33.9 2.5 %collective-permute-start.8 = (bf16[1920,128]{1,0:T(8,128)(2,1)S(1)}, bf16[1920,128]{1,0:T(8,128)(2,1)S(1)}, u32[]{:S(2)}, u32[]{:S(2)}) collective-permute-start(bf16[1920,128]{1,0:T(8,128)(2,1)S(1)} %collective-permute-done.4.first), channel_id=1, source_target_pairs={{0,4},{1,2},{4,8},{5,1},{8,12},{9,5},{12,15},{13,9},{15,11},{14,13... | collective-permute-start | bytes 1474568 | tf_op jit(solution)/shard_map/ppermute | solution.py:314
  36.3 2.8 %collective-permute-done.10.second = bf16[1920,128]{1,0:T(8,128)(2,1)S(1)} collective-permute-done((bf16[1920,128]{1,0:T(8,128)(2,1)S(1)}, bf16[1920,128]{1,0:T(8,128)(2,1)S(1)}, u32[]{:S(2)}, u32[]{:S(2)}) %collective-permute-start.10) | collective-permute-done | bytes 491552 | tf_op jit(solution)/shard_map/ppermute | solution.py:307
  41.0 3.4 %collective-permute-done.8.first = bf16[1920,128]{1,0:T(8,128)(2,1)S(1)} collective-permute-done((bf16[1920,128]{1,0:T(8,128)(2,1)S(1)}, bf16[1920,128]{1,0:T(8,128)(2,1)S(1)}, u32[]{:S(2)}, u32[]{:S(2)}) %collective-permute-start.8) | collective-permute-done | bytes 491552 | tf_op jit(solution)/shard_map/ppermute | solution.py:314
  46.2 8.5 %copy-done = bf16[1792,7168]{1,0:T(8,128)(2,1)} copy-done((bf16[1792,7168]{1,0:T(8,128)(2,1)}, bf16[1792,7168]{1,0:T(8,128)(2,1)S(1)}, u32[]{:S(2)}) %copy-start) | copy-done | bytes 25690136
  59.3 8.3 %copy-done.1 = bf16[1792,7168]{1,0:T(8,128)(2,1)S(1)} copy-done((bf16[1792,7168]{1,0:T(8,128)(2,1)S(1)}, bf16[1792,7168]{1,0:T(8,128)(2,1)}, u32[]{:S(2)}) %copy-start.1) | copy-done | bytes 25690136
  69.2 8.5 %copy-done.2 = bf16[1792,7168]{1,0:T(8,128)(2,1)} copy-done((bf16[1792,7168]{1,0:T(8,128)(2,1)}, bf16[1792,7168]{1,0:T(8,128)(2,1)S(1)}, u32[]{:S(2)}) %copy-start.2) | copy-done | bytes 25690136
  78.1 2.5 %collective-permute-start.14 = (bf16[1920,128]{1,0:T(8,128)(2,1)S(1)}, bf16[1920,128]{1,0:T(8,128)(2,1)S(1)}, u32[]{:S(2)}, u32[]{:S(2)}) collective-permute-start(bf16[1920,128]{1,0:T(8,128)(2,1)S(1)} %get-tuple-element.109.first), channel_id=1, source_target_pairs={{0,4},{1,2},{4,8},{5,1},{8,12},{9,5},{12,15},{13,9},{15,11},{14,13... | collective-permute-start | bytes 1474568 | tf_op jit(solution)/shard_map/ppermute | solution.py:304
  82.2 4.8 %collective-permute-done.14.first = bf16[1920,128]{1,0:T(8,128)(2,1)S(1)} collective-permute-done((bf16[1920,128]{1,0:T(8,128)(2,1)S(1)}, bf16[1920,128]{1,0:T(8,128)(2,1)S(1)}, u32[]{:S(2)}, u32[]{:S(2)}) %collective-permute-start.14) | collective-permute-done | bytes 491552 | tf_op jit(solution)/shard_map/ppermute | solution.py:304
  86.9 2.5 %collective-permute-start.15 = (bf16[1920,128]{1,0:T(8,128)(2,1)S(1)}, bf16[1920,128]{1,0:T(8,128)(2,1)S(1)}, u32[]{:S(2)}, u32[]{:S(2)}) collective-permute-start(bf16[1920,128]{1,0:T(8,128)(2,1)S(1)} %collective-permute-done.14.first), channel_id=1, source_target_pairs={{0,4},{1,2},{4,8},{5,1},{8,12},{9,5},{12,15},{13,9},{15,11},{14,13... | collective-permute-start | bytes 1474568 | tf_op jit(solution)/shard_map/ppermute | solution.py:304
  89.4 8.3 %copy-done.3 = bf16[1792,7168]{1,0:T(8,128)(2,1)S(1)} copy-done((bf16[1792,7168]{1,0:T(8,128)(2,1)S(1)}, bf16[1792,7168]{1,0:T(8,128)(2,1)}, u32[]{:S(2)}) %copy-start.3) | copy-done | bytes 25690136
  106.5 2.3 %collective-permute-done.19.second = bf16[1920,128]{1,0:T(8,128)(2,1)S(1)} collective-permute-done((bf16[1920,128]{1,0:T(8,128)(2,1)S(1)}, bf16[1920,128]{1,0:T(8,128)(2,1)S(1)}, u32[]{:S(2)}, u32[]{:S(2)}) %collective-permute-start.19) | collective-permute-done | bytes 491552 | tf_op jit(solution)/shard_map/ppermute | solution.py:307
  116.3 3.1 %collective-permute-done.24.second = bf16[1920,128]{1,0:T(8,128)(2,1)S(1)} collective-permute-done((bf16[1920,128]{1,0:T(8,128)(2,1)S(1)}, bf16[1920,128]{1,0:T(8,128)(2,1)S(1)}, u32[]{:S(2)}, u32[]{:S(2)}) %collective-permute-start.24) | collective-permute-done | bytes 491552 | tf_op jit(solution)/shard_map/ppermute | solution.py:307
  121.2 3.4 %collective-permute-done.22.first = bf16[1920,128]{1,0:T(8,128)(2,1)S(1)} collective-permute-done((bf16[1920,128]{1,0:T(8,128)(2,1)S(1)}, bf16[1920,128]{1,0:T(8,128)(2,1)S(1)}, u32[]{:S(2)}, u32[]{:S(2)}) %collective-permute-start.22) | collective-permute-done | bytes 491552 | tf_op jit(solution)/shard_map/ppermute | solution.py:314
  126.5 2.3 %collective-permute-start.27 = (f32[1792,128]{1,0:T(8,128)S(1)}, f32[1792,128]{1,0:T(8,128)S(1)}, u32[]{:S(2)}, u32[]{:S(2)}) collective-permute-start(f32[1792,128]{1,0:T(8,128)S(1)} %get-tuple-element.138), channel_id=1, source_target_pairs={{0,1},{1,0},{2,3},{3,2},{4,5},{5,4},{6,7},{7,6},{8,9},{9,8},{10,11... | collective-permute-start | bytes 2752520 | tf_op jit(solution)/shard_map/ppermute | solution.py:23
  137.8 2.9 %collective-permute-done.31 = f32[8,128]{1,0:T(8,128)S(1)} collective-permute-done((f32[8,128]{1,0:T(8,128)S(1)}, f32[8,128]{1,0:T(8,128)S(1)}, u32[]{:S(2)}, u32[]{:S(2)}) %collective-permute-start.31) | collective-permute-done | bytes 4128 | tf_op jit(solution)/shard_map/ppermute | solution.py:32
  141.6 3.7 %collective-permute-done.32 = f32[8,128]{1,0:T(8,128)S(1)} collective-permute-done((f32[8,128]{1,0:T(8,128)S(1)}, f32[8,128]{1,0:T(8,128)S(1)}, u32[]{:S(2)}, u32[]{:S(2)}) %collective-permute-start.32) | collective-permute-done | bytes 4128 | tf_op jit(solution)/shard_map/ppermute | solution.py:32
  (84 shorter events, 55.0 us)
Async XLA Ops:
  3.0 9.3 %collective-permute-start = (bf16[1920,128]{1,0:T(8,128)(2,1)}, bf16[1920,128]{1,0:T(8,128)(2,1)S(1)}, u32[]{:S(2)}, u32[]{:S(2)}) collective-permute-start(bf16[1920,128]{1,0:T(8,128)(2,1)} %shard_map.46.first), channel_id=1, source_target_pairs={{0,4},{1,2},{4,8},{5,1},{8,12},{9,5},{12,15},{13,9},{15,11},{14,13... | collective-permute-start | bytes 1474568 | tf_op jit(solution)/shard_map/ppermute | solution.py:304
  9.6 8.4 %collective-permute-start.3 = (bf16[1920,128]{1,0:T(8,128)(2,1)S(1)}, bf16[1920,128]{1,0:T(8,128)(2,1)S(1)}, u32[]{:S(2)}, u32[]{:S(2)}) collective-permute-start(bf16[1920,128]{1,0:T(8,128)(2,1)S(1)} %get-tuple-element.74.second), channel_id=1, source_target_pairs={{0,4},{1,2},{4,8},{5,1},{8,12},{9,5},{12,15},{13,9},{15,11},{14,13... | collective-permute-start | bytes 1474568 | tf_op jit(solution)/shard_map/ppermute | solution.py:307
  12.3 11.2 %collective-permute-start.2 = (bf16[1920,128]{1,0:T(8,128)(2,1)S(1)}, bf16[1920,128]{1,0:T(8,128)(2,1)S(1)}, u32[]{:S(2)}, u32[]{:S(2)}) collective-permute-start(bf16[1920,128]{1,0:T(8,128)(2,1)S(1)} %collective-permute-done.first), channel_id=1, source_target_pairs={{0,4},{1,2},{4,8},{5,1},{8,12},{9,5},{12,15},{13,9},{15,11},{14,13... | collective-permute-start | bytes 1474568 | tf_op jit(solution)/shard_map/ppermute | solution.py:304
  17.7 5.8 %collective-permute-start.6 = (bf16[1920,128]{1,0:T(8,128)(2,1)S(1)}, bf16[1920,128]{1,0:T(8,128)(2,1)S(1)}, u32[]{:S(2)}, u32[]{:S(2)}) collective-permute-start(bf16[1920,128]{1,0:T(8,128)(2,1)S(1)} %collective-permute-done.first), channel_id=1, source_target_pairs={{0,1},{1,0},{2,3},{3,2},{4,5},{5,4},{6,7},{7,6},{8,9},{9,8},{10,11... | collective-permute-start | bytes 1474568 | tf_op jit(solution)/shard_map/ppermute | solution.py:23
  18.0 7.8 %collective-permute-start.7 = (bf16[1920,128]{1,0:T(8,128)(2,1)S(1)}, bf16[1920,128]{1,0:T(8,128)(2,1)S(1)}, u32[]{:S(2)}, u32[]{:S(2)}) collective-permute-start(bf16[1920,128]{1,0:T(8,128)(2,1)S(1)} %collective-permute-done.3.second), channel_id=1, source_target_pairs={{0,1},{1,0},{2,3},{3,2},{4,5},{5,4},{6,7},{7,6},{8,9},{9,8},{10,11... | collective-permute-start | bytes 1474568 | tf_op jit(solution)/shard_map/ppermute | solution.py:23
  18.3 10.5 %collective-permute-start.5 = (bf16[1920,128]{1,0:T(8,128)(2,1)S(1)}, bf16[1920,128]{1,0:T(8,128)(2,1)S(1)}, u32[]{:S(2)}, u32[]{:S(2)}) collective-permute-start(bf16[1920,128]{1,0:T(8,128)(2,1)S(1)} %collective-permute-done.3.second), channel_id=1, source_target_pairs={{0,4},{1,2},{4,8},{5,1},{8,12},{9,5},{12,15},{13,9},{15,11},{14,13... | collective-permute-start | bytes 1474568 | tf_op jit(solution)/shard_map/ppermute | solution.py:307
  23.5 10.4 %collective-permute-start.4 = (bf16[1920,128]{1,0:T(8,128)(2,1)S(1)}, bf16[1920,128]{1,0:T(8,128)(2,1)S(1)}, u32[]{:S(2)}, u32[]{:S(2)}) collective-permute-start(bf16[1920,128]{1,0:T(8,128)(2,1)S(1)} %collective-permute-done.2.first), channel_id=1, source_target_pairs={{0,4},{1,2},{4,8},{5,1},{8,12},{9,5},{12,15},{13,9},{15,11},{14,13... | collective-permute-start | bytes 1474568 | tf_op jit(solution)/shard_map/ppermute | solution.py:304
  28.7 10.4 %collective-permute-start.10 = (bf16[1920,128]{1,0:T(8,128)(2,1)S(1)}, bf16[1920,128]{1,0:T(8,128)(2,1)S(1)}, u32[]{:S(2)}, u32[]{:S(2)}) collective-permute-start(bf16[1920,128]{1,0:T(8,128)(2,1)S(1)} %collective-permute-done.5.second), channel_id=1, source_target_pairs={{0,4},{1,2},{4,8},{5,1},{8,12},{9,5},{12,15},{13,9},{15,11},{14,13... | collective-permute-start | bytes 1474568 | tf_op jit(solution)/shard_map/ppermute | solution.py:307
  33.8 5.3 %collective-permute-start.9 = (bf16[1920,128]{1,0:T(8,128)(2,1)S(1)}, bf16[1920,128]{1,0:T(8,128)(2,1)S(1)}, u32[]{:S(2)}, u32[]{:S(2)}) collective-permute-start(bf16[1920,128]{1,0:T(8,128)(2,1)S(1)} %collective-permute-done.4.first), channel_id=1, source_target_pairs={{0,1},{1,0},{2,3},{3,2},{4,5},{5,4},{6,7},{7,6},{8,9},{9,8},{10,11... | collective-permute-start | bytes 1474568 | tf_op jit(solution)/shard_map/ppermute | solution.py:23
  33.9 10.5 %collective-permute-start.8 = (bf16[1920,128]{1,0:T(8,128)(2,1)S(1)}, bf16[1920,128]{1,0:T(8,128)(2,1)S(1)}, u32[]{:S(2)}, u32[]{:S(2)}) collective-permute-start(bf16[1920,128]{1,0:T(8,128)(2,1)S(1)} %collective-permute-done.4.first), channel_id=1, source_target_pairs={{0,4},{1,2},{4,8},{5,1},{8,12},{9,5},{12,15},{13,9},{15,11},{14,13... | collective-permute-start | bytes 1474568 | tf_op jit(solution)/shard_map/ppermute | solution.py:314
  54.8 4.5 %collective-permute-start.13 = (f32[1792,128]{1,0:T(8,128)S(1)}, f32[1792,128]{1,0:T(8,128)}, u32[]{:S(2)}, u32[]{:S(2)}) collective-permute-start(f32[1792,128]{1,0:T(8,128)S(1)} %get-tuple-element.105), channel_id=1, source_target_pairs={{0,1},{1,0},{2,3},{3,2},{4,5},{5,4},{6,7},{7,6},{8,9},{9,8},{10,11... | collective-permute-start | bytes 2752520 | tf_op jit(solution)/shard_map/ppermute | solution.py:23
  78.1 8.8 %collective-permute-start.14 = (bf16[1920,128]{1,0:T(8,128)(2,1)S(1)}, bf16[1920,128]{1,0:T(8,128)(2,1)S(1)}, u32[]{:S(2)}, u32[]{:S(2)}) collective-permute-start(bf16[1920,128]{1,0:T(8,128)(2,1)S(1)} %get-tuple-element.109.first), channel_id=1, source_target_pairs={{0,4},{1,2},{4,8},{5,1},{8,12},{9,5},{12,15},{13,9},{15,11},{14,13... | collective-permute-start | bytes 1474568 | tf_op jit(solution)/shard_map/ppermute | solution.py:304
  80.6 19.5 %collective-permute-start.17 = (bf16[1920,128]{1,0:T(8,128)(2,1)S(1)}, bf16[1920,128]{1,0:T(8,128)(2,1)S(1)}, u32[]{:S(2)}, u32[]{:S(2)}) collective-permute-start(bf16[1920,128]{1,0:T(8,128)(2,1)S(1)} %collective-permute-done.16.second), channel_id=1, source_target_pairs={{0,4},{1,2},{4,8},{5,1},{8,12},{9,5},{12,15},{13,9},{15,11},{14,13... | collective-permute-start | bytes 1474568 | tf_op jit(solution)/shard_map/ppermute | solution.py:307
  86.9 17.3 %collective-permute-start.15 = (bf16[1920,128]{1,0:T(8,128)(2,1)S(1)}, bf16[1920,128]{1,0:T(8,128)(2,1)S(1)}, u32[]{:S(2)}, u32[]{:S(2)}) collective-permute-start(bf16[1920,128]{1,0:T(8,128)(2,1)S(1)} %collective-permute-done.14.first), channel_id=1, source_target_pairs={{0,4},{1,2},{4,8},{5,1},{8,12},{9,5},{12,15},{13,9},{15,11},{14,13... | collective-permute-start | bytes 1474568 | tf_op jit(solution)/shard_map/ppermute | solution.py:304
  100.0 4.3 %collective-permute-start.20 = (bf16[1920,128]{1,0:T(8,128)(2,1)S(1)}, bf16[1920,128]{1,0:T(8,128)(2,1)S(1)}, u32[]{:S(2)}, u32[]{:S(2)}) collective-permute-start(bf16[1920,128]{1,0:T(8,128)(2,1)S(1)} %collective-permute-done.14.first), channel_id=1, source_target_pairs={{0,1},{1,0},{2,3},{3,2},{4,5},{5,4},{6,7},{7,6},{8,9},{9,8},{10,11... | collective-permute-start | bytes 1474568 | tf_op jit(solution)/shard_map/ppermute | solution.py:23
  100.1 4.3 %collective-permute-start.21 = (bf16[1920,128]{1,0:T(8,128)(2,1)S(1)}, bf16[1920,128]{1,0:T(8,128)(2,1)S(1)}, u32[]{:S(2)}, u32[]{:S(2)}) collective-permute-start(bf16[1920,128]{1,0:T(8,128)(2,1)S(1)} %collective-permute-done.17.second), channel_id=1, source_target_pairs={{0,1},{1,0},{2,3},{3,2},{4,5},{5,4},{6,7},{7,6},{8,9},{9,8},{10,11... | collective-permute-start | bytes 1474568 | tf_op jit(solution)/shard_map/ppermute | solution.py:23
  100.6 8.3 %collective-permute-start.19 = (bf16[1920,128]{1,0:T(8,128)(2,1)S(1)}, bf16[1920,128]{1,0:T(8,128)(2,1)S(1)}, u32[]{:S(2)}, u32[]{:S(2)}) collective-permute-start(bf16[1920,128]{1,0:T(8,128)(2,1)S(1)} %collective-permute-done.17.second), channel_id=1, source_target_pairs={{0,4},{1,2},{4,8},{5,1},{8,12},{9,5},{12,15},{13,9},{15,11},{14,13... | collective-permute-start | bytes 1474568 | tf_op jit(solution)/shard_map/ppermute | solution.py:307
  104.2 9.8 %collective-permute-start.18 = (bf16[1920,128]{1,0:T(8,128)(2,1)S(1)}, bf16[1920,128]{1,0:T(8,128)(2,1)S(1)}, u32[]{:S(2)}, u32[]{:S(2)}) collective-permute-start(bf16[1920,128]{1,0:T(8,128)(2,1)S(1)} %collective-permute-done.15.first), channel_id=1, source_target_pairs={{0,4},{1,2},{4,8},{5,1},{8,12},{9,5},{12,15},{13,9},{15,11},{14,13... | collective-permute-start | bytes 1474568 | tf_op jit(solution)/shard_map/ppermute | solution.py:304
  108.8 10.5 %collective-permute-start.24 = (bf16[1920,128]{1,0:T(8,128)(2,1)S(1)}, bf16[1920,128]{1,0:T(8,128)(2,1)S(1)}, u32[]{:S(2)}, u32[]{:S(2)}) collective-permute-start(bf16[1920,128]{1,0:T(8,128)(2,1)S(1)} %collective-permute-done.19.second), channel_id=1, source_target_pairs={{0,4},{1,2},{4,8},{5,1},{8,12},{9,5},{12,15},{13,9},{15,11},{14,13... | collective-permute-start | bytes 1474568 | tf_op jit(solution)/shard_map/ppermute | solution.py:307
  114.1 5.3 %collective-permute-start.23 = (bf16[1920,128]{1,0:T(8,128)(2,1)S(1)}, bf16[1920,128]{1,0:T(8,128)(2,1)S(1)}, u32[]{:S(2)}, u32[]{:S(2)}) collective-permute-start(bf16[1920,128]{1,0:T(8,128)(2,1)S(1)} %collective-permute-done.18.first), channel_id=1, source_target_pairs={{0,1},{1,0},{2,3},{3,2},{4,5},{5,4},{6,7},{7,6},{8,9},{9,8},{10,11... | collective-permute-start | bytes 1474568 | tf_op jit(solution)/shard_map/ppermute | solution.py:23
  114.1 10.5 %collective-permute-start.22 = (bf16[1920,128]{1,0:T(8,128)(2,1)S(1)}, bf16[1920,128]{1,0:T(8,128)(2,1)S(1)}, u32[]{:S(2)}, u32[]{:S(2)}) collective-permute-start(bf16[1920,128]{1,0:T(8,128)(2,1)S(1)} %collective-permute-done.18.first), channel_id=1, source_target_pairs={{0,4},{1,2},{4,8},{5,1},{8,12},{9,5},{12,15},{13,9},{15,11},{14,13... | collective-permute-start | bytes 1474568 | tf_op jit(solution)/shard_map/ppermute | solution.py:314
  126.5 4.4 %collective-permute-start.27 = (f32[1792,128]{1,0:T(8,128)S(1)}, f32[1792,128]{1,0:T(8,128)S(1)}, u32[]{:S(2)}, u32[]{:S(2)}) collective-permute-start(f32[1792,128]{1,0:T(8,128)S(1)} %get-tuple-element.138), channel_id=1, source_target_pairs={{0,1},{1,0},{2,3},{3,2},{4,5},{5,4},{6,7},{7,6},{8,9},{9,8},{10,11... | collective-permute-start | bytes 2752520 | tf_op jit(solution)/shard_map/ppermute | solution.py:23
  136.2 4.5 %collective-permute-start.31 = (f32[8,128]{1,0:T(8,128)S(1)}, f32[8,128]{1,0:T(8,128)S(1)}, u32[]{:S(2)}, u32[]{:S(2)}) collective-permute-start(f32[8,128]{1,0:T(8,128)S(1)} %add.23), channel_id=1, source_target_pairs={{0,6},{1,7},{2,4},{3,5},{4,2},{5,3},{6,0},{7,1},{8,14},{9,15},{10,... | collective-permute-start | bytes 12296 | tf_op jit(solution)/shard_map/ppermute | solution.py:32
  140.7 4.5 %collective-permute-start.32 = (f32[8,128]{1,0:T(8,128)S(1)}, f32[8,128]{1,0:T(8,128)S(1)}, u32[]{:S(2)}, u32[]{:S(2)}) collective-permute-start(f32[8,128]{1,0:T(8,128)S(1)} %add_add_fusion), channel_id=1, source_target_pairs={{0,8},{1,9},{2,10},{3,11},{4,12},{5,13},{6,14},{7,15},{8,0},{9,1},... | collective-permute-start | bytes 12296 | tf_op jit(solution)/shard_map/ppermute | solution.py:32
  (18 other events, 123.4 us)

commit v2 on v0

--- a/solution.py
+++ b/solution.py
@@ -26,10 +26,8 @@
     devices = 2 * count
     unit = 1
     while unit < devices:
-        size = 2 if unit == 1 else min(4, devices // unit)
-        swaps = [[(i, i ^ k * unit) for i in range(devices)] for k in range(1, size)]
-        value += sum(lax.ppermute(value, AXES, pairs) for pairs in swaps)
-        unit *= size
+        value += lax.ppermute(value, AXES, [(i, i ^ unit) for i in range(devices)])
+        unit *= 2
     return value
 
 

time: 115 us -> 115 us (level)
    ppermute x5 -> x4, waiting for transfers between devices: 7.03 us -> 6.07 us  [sum_part(): value += lax.ppermute(value, AXES, [(i, i ^ unit) for i in range(devices)])]
    ppermute x5 -> x4, starting transfers between devices: 7.27 us -> 7.75 us  [sum_part(): value += lax.ppermute(value, AXES, [(i, i ^ unit) for i in range(devices)])]
  transfers between devices with their start and end apart: 33 -> 32, of which waited for: 22 -> 22; matrix products, arithmetic and copies ran while one was open for 0% -> 0% of each run, Pallas kernels for 20% -> 20%
where the time goes in v2:
time: 115 us; the launch traced here: 114 us
  starting transfers between devices  46.1 us (40%)
  waiting for transfers between devices  39.1 us (34%)
  Pallas kernels  25 us (22%)
  local copies, waits for them, and re-layouts  3.3 us (3%)
    pallas_call x14, Pallas kernels, product(): pl.pallas_call(functools.partial(product_kernel, ring, slot, loads, with_...  19.6 us
    ppermute x6, starting transfers between devices, ring_apply(): came = lax.ppermute(after(first, acc[:1]), AXES, ring.shift())  14.6 us
    ppermute x6, starting transfers between devices, ring_apply(): second = lax.ppermute(after(second, acc[:1]), AXES, ring.shift())  12.9 us
    ppermute x14, waiting for transfers between devices, swap(): lax.ppermute(value, axis, [(i, i ^ distance) for i in range(lax.axis_size...  11.6 us
    ppermute x4, starting transfers between devices, sum_part(): value += lax.ppermute(value, AXES, [(i, i ^ unit) for i in range(devices)])  7.75 us
    ppermute x6, waiting for transfers between devices, ring_apply(): came = lax.ppermute(after(first, acc[:1]), AXES, ring.shift())  7.45 us
    ppermute x6, waiting for transfers between devices, ring_apply(): second = lax.ppermute(after(second, acc[:1]), AXES, ring.shift())  7.12 us
    ppermute x2, waiting for transfers between devices, ring_apply(): first = lax.ppermute(after(first, acc[:1]), AXES, ring.shift())  6.8 us
  transfers between devices with their start and end apart: 32, of which 22 were waited for; matrix products, arithmetic and copies ran while one was open for 0% of the time, Pallas kernels for 20%

profile of v2, /device:TPU:0, one launch (start us, length us, event | category | flops | bytes accessed | tf_op | source)
XLA Modules:
  0.0 114.4 jit_solution(1500642804386039267)
XLA Ops:
  3.9 2.6 %collective-permute-start = (bf16[1920,128]{1,0:T(8,128)(2,1)S(1)}, bf16[1920,128]{1,0:T(8,128)(2,1)S(1)}, u32[]{:S(2)}, u32[]{:S(2)}) collective-permute-start(bf16[1920,128]{1,0:T(8,128)(2,1)S(1)} %shard_map.46.first), channel_id=1, source_target_pairs={{0,4},{1,2},{4,8},{5,1},{8,12},{9,5},{12,15},{13,9},{15,11},{14,13... | collective-permute-start | bytes 1474568 | tf_op jit(solution)/shard_map/ppermute | solution.py:301
  7.5 3.0 %shard_map.47 = (bf16[1792,7168]{1,0:T(8,128)(2,1)S(1)}, bf16[1792,128]{1,0:T(8,128)(2,1)S(1)}, bf16[1920,128]{1,0:T(8,128)(2,1)S(1)}) custom-call(bf16[1792,7168]{1,0:T(8,128)(2,1)} %refs_2_.3, bf16[128,1792]{1,0:T(8,128)(2,1)S(1)} %copy-done.1, bf16[1920,128]{1,0:T(8,128)(2,1)S(1)} %collective-permute-done.1.second), custom_call_target="tpu_custom_call", output_to_operand_aliasing={{2}: (2, {})} | custom-call | tf_op jit(solution)/shard_map/pallas_call | solution.py:165
  13.0 2.4 %collective-permute-start.2 = (bf16[1920,128]{1,0:T(8,128)(2,1)S(1)}, bf16[1920,128]{1,0:T(8,128)(2,1)S(1)}, u32[]{:S(2)}, u32[]{:S(2)}) collective-permute-start(bf16[1920,128]{1,0:T(8,128)(2,1)S(1)} %collective-permute-done.first), channel_id=1, source_target_pairs={{0,4},{1,2},{4,8},{5,1},{8,12},{9,5},{12,15},{13,9},{15,11},{14,13... | collective-permute-start | bytes 1474568 | tf_op jit(solution)/shard_map/ppermute | solution.py:301
  15.4 3.0 %shard_map.48 = (f32[1792,128]{1,0:T(8,128)S(1)}, f32[1792,128]{1,0:T(8,128)S(1)}, bf16[1792,7168]{1,0:T(8,128)(2,1)S(1)}, f32[8,128]{1,0:T(8,128)S(1)}) custom-call(bf16[1920,128]{1,0:T(8,128)(2,1)S(1)} %shard_map.46.first, bf16[1920,128]{1,0:T(8,128)(2,1)S(1)} %get-tuple-element.74.second, ...), custom_call_target="tpu_custom_call", output_to_operand_aliasing={{2}: (5, {})} | custom-call | flops 1644167168 | bytes 6422528 | tf_op jit(solution)/shard_map/pallas_call | solution.py:256
  21.2 2.9 %shard_map.49 = (f32[1792,128]{1,0:T(8,128)S(1)}, f32[1792,128]{1,0:T(8,128)S(1)}, bf16[1792,7168]{1,0:T(8,128)(2,1)S(1)}) custom-call(bf16[1920,128]{1,0:T(8,128)(2,1)S(1)} %collective-permute-done.first, bf16[1920,128]{1,0:T(8,128)(2,1)S(1)} %collective-permute-done.3.second, ...), custom_call_target="tpu_custom_call", output_to_operand_aliasing={{0}: (3, {}), {1}: (4, {}), {2}: (6, {})} | custom-call | flops 1644167168 | bytes 6422528 | tf_op jit(solution)/shard_map/pallas_call | solution.py:256
  24.1 2.3 %collective-permute-start.4 = (bf16[1920,128]{1,0:T(8,128)(2,1)S(1)}, bf16[1920,128]{1,0:T(8,128)(2,1)S(1)}, u32[]{:S(2)}, u32[]{:S(2)}) collective-permute-start(bf16[1920,128]{1,0:T(8,128)(2,1)S(1)} %collective-permute-done.2.first), channel_id=1, source_target_pairs={{0,4},{1,2},{4,8},{5,1},{8,12},{9,5},{12,15},{13,9},{15,11},{14,13... | collective-permute-start | bytes 1474568 | tf_op jit(solution)/shard_map/ppermute | solution.py:301
  26.5 2.9 %shard_map.50 = (f32[1792,128]{1,0:T(8,128)S(1)}, f32[1792,128]{1,0:T(8,128)S(1)}, bf16[1792,7168]{1,0:T(8,128)(2,1)S(1)}) custom-call(bf16[1920,128]{1,0:T(8,128)(2,1)S(1)} %collective-permute-done.6.first, bf16[1920,128]{1,0:T(8,128)(2,1)S(1)} %collective-permute-done.7.second, ...), custom_call_target="tpu_custom_call", output_to_operand_aliasing={{0}: (3, {}), {1}: (4, {}), {2}: (6, {})} | custom-call | flops 493250144 | bytes 1926758 | tf_op jit(solution)/shard_map/pallas_call | solution.py:256
  29.4 2.3 %collective-permute-start.10 = (bf16[1920,128]{1,0:T(8,128)(2,1)S(1)}, bf16[1920,128]{1,0:T(8,128)(2,1)S(1)}, u32[]{:S(2)}, u32[]{:S(2)}) collective-permute-start(bf16[1920,128]{1,0:T(8,128)(2,1)S(1)} %collective-permute-done.5.second), channel_id=1, source_target_pairs={{0,4},{1,2},{4,8},{5,1},{8,12},{9,5},{12,15},{13,9},{15,11},{14,13... | collective-permute-start | bytes 1474568 | tf_op jit(solution)/shard_map/ppermute | solution.py:304
  34.6 2.4 %collective-permute-start.8 = (bf16[1920,128]{1,0:T(8,128)(2,1)S(1)}, bf16[1920,128]{1,0:T(8,128)(2,1)S(1)}, u32[]{:S(2)}, u32[]{:S(2)}) collective-permute-start(bf16[1920,128]{1,0:T(8,128)(2,1)S(1)} %collective-permute-done.4.first), channel_id=1, source_target_pairs={{0,4},{1,2},{4,8},{5,1},{8,12},{9,5},{12,15},{13,9},{15,11},{14,13... | collective-permute-start | bytes 1474568 | tf_op jit(solution)/shard_map/ppermute | solution.py:311
  37.0 2.9 %collective-permute-done.10.second = bf16[1920,128]{1,0:T(8,128)(2,1)S(1)} collective-permute-done((bf16[1920,128]{1,0:T(8,128)(2,1)S(1)}, bf16[1920,128]{1,0:T(8,128)(2,1)S(1)}, u32[]{:S(2)}, u32[]{:S(2)}) %collective-permute-start.10) | collective-permute-done | bytes 491552 | tf_op jit(solution)/shard_map/ppermute | solution.py:304
  41.8 3.4 %collective-permute-done.8.first = bf16[1920,128]{1,0:T(8,128)(2,1)S(1)} collective-permute-done((bf16[1920,128]{1,0:T(8,128)(2,1)S(1)}, bf16[1920,128]{1,0:T(8,128)(2,1)S(1)}, u32[]{:S(2)}, u32[]{:S(2)}) %collective-permute-start.8) | collective-permute-done | bytes 491552 | tf_op jit(solution)/shard_map/ppermute | solution.py:311
  47.0 2.3 %collective-permute-start.13 = (f32[1792,128]{1,0:T(8,128)S(1)}, f32[1792,128]{1,0:T(8,128)S(1)}, u32[]{:S(2)}, u32[]{:S(2)}) collective-permute-start(f32[1792,128]{1,0:T(8,128)S(1)} %get-tuple-element.105), channel_id=1, source_target_pairs={{0,1},{1,0},{2,3},{3,2},{4,5},{5,4},{6,7},{7,6},{8,9},{9,8},{10,11... | collective-permute-start | bytes 2752520 | tf_op jit(solution)/shard_map/ppermute | solution.py:22
  52.3 2.3 %collective-permute-start.14 = (bf16[1920,128]{1,0:T(8,128)(2,1)S(1)}, bf16[1920,128]{1,0:T(8,128)(2,1)S(1)}, u32[]{:S(2)}, u32[]{:S(2)}) collective-permute-start(bf16[1920,128]{1,0:T(8,128)(2,1)S(1)} %get-tuple-element.109.first), channel_id=1, source_target_pairs={{0,4},{1,2},{4,8},{5,1},{8,12},{9,5},{12,15},{13,9},{15,11},{14,13... | collective-permute-start | bytes 1474568 | tf_op jit(solution)/shard_map/ppermute | solution.py:301
  56.3 4.7 %collective-permute-done.14.first = bf16[1920,128]{1,0:T(8,128)(2,1)S(1)} collective-permute-done((bf16[1920,128]{1,0:T(8,128)(2,1)S(1)}, bf16[1920,128]{1,0:T(8,128)(2,1)S(1)}, u32[]{:S(2)}, u32[]{:S(2)}) %collective-permute-start.14) | collective-permute-done | bytes 491552 | tf_op jit(solution)/shard_map/ppermute | solution.py:301
  61.0 2.5 %collective-permute-start.15 = (bf16[1920,128]{1,0:T(8,128)(2,1)S(1)}, bf16[1920,128]{1,0:T(8,128)(2,1)S(1)}, u32[]{:S(2)}, u32[]{:S(2)}) collective-permute-start(bf16[1920,128]{1,0:T(8,128)(2,1)S(1)} %collective-permute-done.14.first), channel_id=1, source_target_pairs={{0,4},{1,2},{4,8},{5,1},{8,12},{9,5},{12,15},{13,9},{15,11},{14,13... | collective-permute-start | bytes 1474568 | tf_op jit(solution)/shard_map/ppermute | solution.py:301
  66.3 2.4 %collective-permute-start.19 = (bf16[1920,128]{1,0:T(8,128)(2,1)S(1)}, bf16[1920,128]{1,0:T(8,128)(2,1)S(1)}, u32[]{:S(2)}, u32[]{:S(2)}) collective-permute-start(bf16[1920,128]{1,0:T(8,128)(2,1)S(1)} %collective-permute-done.17.second), channel_id=1, source_target_pairs={{0,4},{1,2},{4,8},{5,1},{8,12},{9,5},{12,15},{13,9},{15,11},{14,13... | collective-permute-start | bytes 1474568 | tf_op jit(solution)/shard_map/ppermute | solution.py:304
  71.5 2.5 %collective-permute-start.18 = (bf16[1920,128]{1,0:T(8,128)(2,1)S(1)}, bf16[1920,128]{1,0:T(8,128)(2,1)S(1)}, u32[]{:S(2)}, u32[]{:S(2)}) collective-permute-start(bf16[1920,128]{1,0:T(8,128)(2,1)S(1)} %collective-permute-done.15.first), channel_id=1, source_target_pairs={{0,4},{1,2},{4,8},{5,1},{8,12},{9,5},{12,15},{13,9},{15,11},{14,13... | collective-permute-start | bytes 1474568 | tf_op jit(solution)/shard_map/ppermute | solution.py:301
  76.8 2.5 %collective-permute-start.24 = (bf16[1920,128]{1,0:T(8,128)(2,1)S(1)}, bf16[1920,128]{1,0:T(8,128)(2,1)S(1)}, u32[]{:S(2)}, u32[]{:S(2)}) collective-permute-start(bf16[1920,128]{1,0:T(8,128)(2,1)S(1)} %collective-permute-done.19.second), channel_id=1, source_target_pairs={{0,4},{1,2},{4,8},{5,1},{8,12},{9,5},{12,15},{13,9},{15,11},{14,13... | collective-permute-start | bytes 1474568 | tf_op jit(solution)/shard_map/ppermute | solution.py:304
  82.1 2.5 %collective-permute-start.22 = (bf16[1920,128]{1,0:T(8,128)(2,1)S(1)}, bf16[1920,128]{1,0:T(8,128)(2,1)S(1)}, u32[]{:S(2)}, u32[]{:S(2)}) collective-permute-start(bf16[1920,128]{1,0:T(8,128)(2,1)S(1)} %collective-permute-done.18.first), channel_id=1, source_target_pairs={{0,4},{1,2},{4,8},{5,1},{8,12},{9,5},{12,15},{13,9},{15,11},{14,13... | collective-permute-start | bytes 1474568 | tf_op jit(solution)/shard_map/ppermute | solution.py:311
  84.5 2.8 %collective-permute-done.24.second = bf16[1920,128]{1,0:T(8,128)(2,1)S(1)} collective-permute-done((bf16[1920,128]{1,0:T(8,128)(2,1)S(1)}, bf16[1920,128]{1,0:T(8,128)(2,1)S(1)}, u32[]{:S(2)}, u32[]{:S(2)}) %collective-permute-start.24) | collective-permute-done | bytes 491552 | tf_op jit(solution)/shard_map/ppermute | solution.py:304
  89.2 3.4 %collective-permute-done.22.first = bf16[1920,128]{1,0:T(8,128)(2,1)S(1)} collective-permute-done((bf16[1920,128]{1,0:T(8,128)(2,1)S(1)}, bf16[1920,128]{1,0:T(8,128)(2,1)S(1)}, u32[]{:S(2)}, u32[]{:S(2)}) %collective-permute-start.22) | collective-permute-done | bytes 491552 | tf_op jit(solution)/shard_map/ppermute | solution.py:311
  94.4 2.3 %collective-permute-start.27 = (f32[1792,128]{1,0:T(8,128)S(1)}, f32[1792,128]{1,0:T(8,128)S(1)}, u32[]{:S(2)}, u32[]{:S(2)}) collective-permute-start(f32[1792,128]{1,0:T(8,128)S(1)} %get-tuple-element.138), channel_id=1, source_target_pairs={{0,1},{1,0},{2,3},{3,2},{4,5},{5,4},{6,7},{7,6},{8,9},{9,8},{10,11... | collective-permute-start | bytes 2752520 | tf_op jit(solution)/shard_map/ppermute | solution.py:22
  104.1 2.4 %collective-permute-start.30 = (f32[8,128]{1,0:T(8,128)S(1)}, f32[8,128]{1,0:T(8,128)S(1)}, u32[]{:S(2)}, u32[]{:S(2)}) collective-permute-start(f32[8,128]{1,0:T(8,128)S(1)} %add.21), channel_id=1, source_target_pairs={{0,4},{1,5},{2,6},{3,7},{4,0},{5,1},{6,2},{7,3},{8,12},{9,13},{10,... | collective-permute-start | bytes 12296 | tf_op jit(solution)/shard_map/ppermute | solution.py:29
  108.1 3.4 %collective-permute-start.31 = (f32[8,128]{1,0:T(8,128)S(1)}, f32[8,128]{1,0:T(8,128)S(1)}, u32[]{:S(2)}, u32[]{:S(2)}) collective-permute-start(f32[8,128]{1,0:T(8,128)S(1)} %add.22), channel_id=1, source_target_pairs={{0,8},{1,9},{2,10},{3,11},{4,12},{5,13},{6,14},{7,15},{8,0},{9,1},... | collective-permute-start | bytes 12296 | tf_op jit(solution)/shard_map/ppermute | solution.py:29
  (75 shorter events, 48.1 us)
Async XLA Ops:
  3.9 9.1 %collective-permute-start = (bf16[1920,128]{1,0:T(8,128)(2,1)S(1)}, bf16[1920,128]{1,0:T(8,128)(2,1)S(1)}, u32[]{:S(2)}, u32[]{:S(2)}) collective-permute-start(bf16[1920,128]{1,0:T(8,128)(2,1)S(1)} %shard_map.46.first), channel_id=1, source_target_pairs={{0,4},{1,2},{4,8},{5,1},{8,12},{9,5},{12,15},{13,9},{15,11},{14,13... | collective-permute-start | bytes 1474568 | tf_op jit(solution)/shard_map/ppermute | solution.py:301
  10.5 8.3 %collective-permute-start.3 = (bf16[1920,128]{1,0:T(8,128)(2,1)S(1)}, bf16[1920,128]{1,0:T(8,128)(2,1)S(1)}, u32[]{:S(2)}, u32[]{:S(2)}) collective-permute-start(bf16[1920,128]{1,0:T(8,128)(2,1)S(1)} %get-tuple-element.74.second), channel_id=1, source_target_pairs={{0,4},{1,2},{4,8},{5,1},{8,12},{9,5},{12,15},{13,9},{15,11},{14,13... | collective-permute-start | bytes 1474568 | tf_op jit(solution)/shard_map/ppermute | solution.py:304
  13.0 11.1 %collective-permute-start.2 = (bf16[1920,128]{1,0:T(8,128)(2,1)S(1)}, bf16[1920,128]{1,0:T(8,128)(2,1)S(1)}, u32[]{:S(2)}, u32[]{:S(2)}) collective-permute-start(bf16[1920,128]{1,0:T(8,128)(2,1)S(1)} %collective-permute-done.first), channel_id=1, source_target_pairs={{0,4},{1,2},{4,8},{5,1},{8,12},{9,5},{12,15},{13,9},{15,11},{14,13... | collective-permute-start | bytes 1474568 | tf_op jit(solution)/shard_map/ppermute | solution.py:301
  18.4 5.7 %collective-permute-start.6 = (bf16[1920,128]{1,0:T(8,128)(2,1)S(1)}, bf16[1920,128]{1,0:T(8,128)(2,1)S(1)}, u32[]{:S(2)}, u32[]{:S(2)}) collective-permute-start(bf16[1920,128]{1,0:T(8,128)(2,1)S(1)} %collective-permute-done.first), channel_id=1, source_target_pairs={{0,1},{1,0},{2,3},{3,2},{4,5},{5,4},{6,7},{7,6},{8,9},{9,8},{10,11... | collective-permute-start | bytes 1474568 | tf_op jit(solution)/shard_map/ppermute | solution.py:22
  18.8 7.6 %collective-permute-start.7 = (bf16[1920,128]{1,0:T(8,128)(2,1)S(1)}, bf16[1920,128]{1,0:T(8,128)(2,1)S(1)}, u32[]{:S(2)}, u32[]{:S(2)}) collective-permute-start(bf16[1920,128]{1,0:T(8,128)(2,1)S(1)} %collective-permute-done.3.second), channel_id=1, source_target_pairs={{0,1},{1,0},{2,3},{3,2},{4,5},{5,4},{6,7},{7,6},{8,9},{9,8},{10,11... | collective-permute-start | bytes 1474568 | tf_op jit(solution)/shard_map/ppermute | solution.py:22
  19.0 10.4 %collective-permute-start.5 = (bf16[1920,128]{1,0:T(8,128)(2,1)S(1)}, bf16[1920,128]{1,0:T(8,128)(2,1)S(1)}, u32[]{:S(2)}, u32[]{:S(2)}) collective-permute-start(bf16[1920,128]{1,0:T(8,128)(2,1)S(1)} %collective-permute-done.3.second), channel_id=1, source_target_pairs={{0,4},{1,2},{4,8},{5,1},{8,12},{9,5},{12,15},{13,9},{15,11},{14,13... | collective-permute-start | bytes 1474568 | tf_op jit(solution)/shard_map/ppermute | solution.py:304
  24.1 10.5 %collective-permute-start.4 = (bf16[1920,128]{1,0:T(8,128)(2,1)S(1)}, bf16[1920,128]{1,0:T(8,128)(2,1)S(1)}, u32[]{:S(2)}, u32[]{:S(2)}) collective-permute-start(bf16[1920,128]{1,0:T(8,128)(2,1)S(1)} %collective-permute-done.2.first), channel_id=1, source_target_pairs={{0,4},{1,2},{4,8},{5,1},{8,12},{9,5},{12,15},{13,9},{15,11},{14,13... | collective-permute-start | bytes 1474568 | tf_op jit(solution)/shard_map/ppermute | solution.py:301
  29.4 10.5 %collective-permute-start.10 = (bf16[1920,128]{1,0:T(8,128)(2,1)S(1)}, bf16[1920,128]{1,0:T(8,128)(2,1)S(1)}, u32[]{:S(2)}, u32[]{:S(2)}) collective-permute-start(bf16[1920,128]{1,0:T(8,128)(2,1)S(1)} %collective-permute-done.5.second), channel_id=1, source_target_pairs={{0,4},{1,2},{4,8},{5,1},{8,12},{9,5},{12,15},{13,9},{15,11},{14,13... | collective-permute-start | bytes 1474568 | tf_op jit(solution)/shard_map/ppermute | solution.py:304
  34.6 5.3 %collective-permute-start.9 = (bf16[1920,128]{1,0:T(8,128)(2,1)S(1)}, bf16[1920,128]{1,0:T(8,128)(2,1)S(1)}, u32[]{:S(2)}, u32[]{:S(2)}) collective-permute-start(bf16[1920,128]{1,0:T(8,128)(2,1)S(1)} %collective-permute-done.4.first), channel_id=1, source_target_pairs={{0,1},{1,0},{2,3},{3,2},{4,5},{5,4},{6,7},{7,6},{8,9},{9,8},{10,11... | collective-permute-start | bytes 1474568 | tf_op jit(solution)/shard_map/ppermute | solution.py:22
  34.6 10.5 %collective-permute-start.8 = (bf16[1920,128]{1,0:T(8,128)(2,1)S(1)}, bf16[1920,128]{1,0:T(8,128)(2,1)S(1)}, u32[]{:S(2)}, u32[]{:S(2)}) collective-permute-start(bf16[1920,128]{1,0:T(8,128)(2,1)S(1)} %collective-permute-done.4.first), channel_id=1, source_target_pairs={{0,4},{1,2},{4,8},{5,1},{8,12},{9,5},{12,15},{13,9},{15,11},{14,13... | collective-permute-start | bytes 1474568 | tf_op jit(solution)/shard_map/ppermute | solution.py:311
  47.0 4.4 %collective-permute-start.13 = (f32[1792,128]{1,0:T(8,128)S(1)}, f32[1792,128]{1,0:T(8,128)S(1)}, u32[]{:S(2)}, u32[]{:S(2)}) collective-permute-start(f32[1792,128]{1,0:T(8,128)S(1)} %get-tuple-element.105), channel_id=1, source_target_pairs={{0,1},{1,0},{2,3},{3,2},{4,5},{5,4},{6,7},{7,6},{8,9},{9,8},{10,11... | collective-permute-start | bytes 2752520 | tf_op jit(solution)/shard_map/ppermute | solution.py:22
  52.3 8.7 %collective-permute-start.14 = (bf16[1920,128]{1,0:T(8,128)(2,1)S(1)}, bf16[1920,128]{1,0:T(8,128)(2,1)S(1)}, u32[]{:S(2)}, u32[]{:S(2)}) collective-permute-start(bf16[1920,128]{1,0:T(8,128)(2,1)S(1)} %get-tuple-element.109.first), channel_id=1, source_target_pairs={{0,4},{1,2},{4,8},{5,1},{8,12},{9,5},{12,15},{13,9},{15,11},{14,13... | collective-permute-start | bytes 1474568 | tf_op jit(solution)/shard_map/ppermute | solution.py:301
  54.6 11.6 %collective-permute-start.17 = (bf16[1920,128]{1,0:T(8,128)(2,1)S(1)}, bf16[1920,128]{1,0:T(8,128)(2,1)S(1)}, u32[]{:S(2)}, u32[]{:S(2)}) collective-permute-start(bf16[1920,128]{1,0:T(8,128)(2,1)S(1)} %collective-permute-done.16.second), channel_id=1, source_target_pairs={{0,4},{1,2},{4,8},{5,1},{8,12},{9,5},{12,15},{13,9},{15,11},{14,13... | collective-permute-start | bytes 1474568 | tf_op jit(solution)/shard_map/ppermute | solution.py:304
  61.0 10.5 %collective-permute-start.15 = (bf16[1920,128]{1,0:T(8,128)(2,1)S(1)}, bf16[1920,128]{1,0:T(8,128)(2,1)S(1)}, u32[]{:S(2)}, u32[]{:S(2)}) collective-permute-start(bf16[1920,128]{1,0:T(8,128)(2,1)S(1)} %collective-permute-done.14.first), channel_id=1, source_target_pairs={{0,4},{1,2},{4,8},{5,1},{8,12},{9,5},{12,15},{13,9},{15,11},{14,13... | collective-permute-start | bytes 1474568 | tf_op jit(solution)/shard_map/ppermute | solution.py:301
  65.7 8.3 %collective-permute-start.20 = (bf16[1920,128]{1,0:T(8,128)(2,1)S(1)}, bf16[1920,128]{1,0:T(8,128)(2,1)S(1)}, u32[]{:S(2)}, u32[]{:S(2)}) collective-permute-start(bf16[1920,128]{1,0:T(8,128)(2,1)S(1)} %collective-permute-done.14.first), channel_id=1, source_target_pairs={{0,1},{1,0},{2,3},{3,2},{4,5},{5,4},{6,7},{7,6},{8,9},{9,8},{10,11... | collective-permute-start | bytes 1474568 | tf_op jit(solution)/shard_map/ppermute | solution.py:22
  66.2 7.8 %collective-permute-start.21 = (bf16[1920,128]{1,0:T(8,128)(2,1)S(1)}, bf16[1920,128]{1,0:T(8,128)(2,1)S(1)}, u32[]{:S(2)}, u32[]{:S(2)}) collective-permute-start(bf16[1920,128]{1,0:T(8,128)(2,1)S(1)} %collective-permute-done.17.second), channel_id=1, source_target_pairs={{0,1},{1,0},{2,3},{3,2},{4,5},{5,4},{6,7},{7,6},{8,9},{9,8},{10,11... | collective-permute-start | bytes 1474568 | tf_op jit(solution)/shard_map/ppermute | solution.py:22
  66.3 10.5 %collective-permute-start.19 = (bf16[1920,128]{1,0:T(8,128)(2,1)S(1)}, bf16[1920,128]{1,0:T(8,128)(2,1)S(1)}, u32[]{:S(2)}, u32[]{:S(2)}) collective-permute-start(bf16[1920,128]{1,0:T(8,128)(2,1)S(1)} %collective-permute-done.17.second), channel_id=1, source_target_pairs={{0,4},{1,2},{4,8},{5,1},{8,12},{9,5},{12,15},{13,9},{15,11},{14,13... | collective-permute-start | bytes 1474568 | tf_op jit(solution)/shard_map/ppermute | solution.py:304
  71.5 10.5 %collective-permute-start.18 = (bf16[1920,128]{1,0:T(8,128)(2,1)S(1)}, bf16[1920,128]{1,0:T(8,128)(2,1)S(1)}, u32[]{:S(2)}, u32[]{:S(2)}) collective-permute-start(bf16[1920,128]{1,0:T(8,128)(2,1)S(1)} %collective-permute-done.15.first), channel_id=1, source_target_pairs={{0,4},{1,2},{4,8},{5,1},{8,12},{9,5},{12,15},{13,9},{15,11},{14,13... | collective-permute-start | bytes 1474568 | tf_op jit(solution)/shard_map/ppermute | solution.py:301
  76.8 10.5 %collective-permute-start.24 = (bf16[1920,128]{1,0:T(8,128)(2,1)S(1)}, bf16[1920,128]{1,0:T(8,128)(2,1)S(1)}, u32[]{:S(2)}, u32[]{:S(2)}) collective-permute-start(bf16[1920,128]{1,0:T(8,128)(2,1)S(1)} %collective-permute-done.19.second), channel_id=1, source_target_pairs={{0,4},{1,2},{4,8},{5,1},{8,12},{9,5},{12,15},{13,9},{15,11},{14,13... | collective-permute-start | bytes 1474568 | tf_op jit(solution)/shard_map/ppermute | solution.py:304
  82.0 5.3 %collective-permute-start.23 = (bf16[1920,128]{1,0:T(8,128)(2,1)S(1)}, bf16[1920,128]{1,0:T(8,128)(2,1)S(1)}, u32[]{:S(2)}, u32[]{:S(2)}) collective-permute-start(bf16[1920,128]{1,0:T(8,128)(2,1)S(1)} %collective-permute-done.18.first), channel_id=1, source_target_pairs={{0,1},{1,0},{2,3},{3,2},{4,5},{5,4},{6,7},{7,6},{8,9},{9,8},{10,11... | collective-permute-start | bytes 1474568 | tf_op jit(solution)/shard_map/ppermute | solution.py:22
  82.1 10.5 %collective-permute-start.22 = (bf16[1920,128]{1,0:T(8,128)(2,1)S(1)}, bf16[1920,128]{1,0:T(8,128)(2,1)S(1)}, u32[]{:S(2)}, u32[]{:S(2)}) collective-permute-start(bf16[1920,128]{1,0:T(8,128)(2,1)S(1)} %collective-permute-done.18.first), channel_id=1, source_target_pairs={{0,4},{1,2},{4,8},{5,1},{8,12},{9,5},{12,15},{13,9},{15,11},{14,13... | collective-permute-start | bytes 1474568 | tf_op jit(solution)/shard_map/ppermute | solution.py:311
  94.4 4.4 %collective-permute-start.27 = (f32[1792,128]{1,0:T(8,128)S(1)}, f32[1792,128]{1,0:T(8,128)S(1)}, u32[]{:S(2)}, u32[]{:S(2)}) collective-permute-start(f32[1792,128]{1,0:T(8,128)S(1)} %get-tuple-element.138), channel_id=1, source_target_pairs={{0,1},{1,0},{2,3},{3,2},{4,5},{5,4},{6,7},{7,6},{8,9},{9,8},{10,11... | collective-permute-start | bytes 2752520 | tf_op jit(solution)/shard_map/ppermute | solution.py:22
  104.1 4.0 %collective-permute-start.30 = (f32[8,128]{1,0:T(8,128)S(1)}, f32[8,128]{1,0:T(8,128)S(1)}, u32[]{:S(2)}, u32[]{:S(2)}) collective-permute-start(f32[8,128]{1,0:T(8,128)S(1)} %add.21), channel_id=1, source_target_pairs={{0,4},{1,5},{2,6},{3,7},{4,0},{5,1},{6,2},{7,3},{8,12},{9,13},{10,... | collective-permute-start | bytes 12296 | tf_op jit(solution)/shard_map/ppermute | solution.py:29
  108.1 5.0 %collective-permute-start.31 = (f32[8,128]{1,0:T(8,128)S(1)}, f32[8,128]{1,0:T(8,128)S(1)}, u32[]{:S(2)}, u32[]{:S(2)}) collective-permute-start(f32[8,128]{1,0:T(8,128)S(1)} %add.22), channel_id=1, source_target_pairs={{0,8},{1,9},{2,10},{3,11},{4,12},{5,13},{6,14},{7,15},{8,0},{9,1},... | collective-permute-start | bytes 12296 | tf_op jit(solution)/shard_map/ppermute | solution.py:29
  (13 other events, 55.0 us)

commit v3 on v2

--- a/solution.py
+++ b/solution.py
@@ -323,13 +323,14 @@
     ).astype(message.dtype)
 
 
-def head_kernel(weights, blocks, acts, message):
+def head_kernel(weights, blocks, acts, message, kept_acts):
     rows = weights.shape[0]
     for block in range(rows // BLK):
         here = slice(block * BLK, (block + 1) * BLK)
         dense = weights[here, :]
         message[here, :] = (blocks[block : block + 1, :] * dense - dense).astype(message.dtype)
     put_message(message, acts, rows)
+    kept_acts[...] = acts[...]
 
 
 def turn_kernel(own, received, blocks, acts, _, grad, message, __):
@@ -471,7 +472,10 @@
     letter = jax.ShapeDtypeStruct((row_block + samples, width), jnp.bfloat16)
     eight = jax.ShapeDtypeStruct((8, width), jnp.float32)
 
-    (message,) = call_whole(head_kernel, [letter], weights, blocks, activations)
+    samples_shape = jax.ShapeDtypeStruct(activations.shape, activations.dtype)
+    message, activations = call_whole(
+        head_kernel, [letter, samples_shape], weights, blocks, activations
+    )
     across = None
 
     def load(second):

time: 115 us -> 114 us (level)
    unnamed x10 -> x6, local copies, waits for them, and re-layouts: 3.22 us -> 2.2 us
  transfers between devices with their start and end apart: 32 -> 32, of which waited for: 22 -> 21; matrix products, arithmetic and copies ran while one was open for 0% -> 0% of each run, Pallas kernels for 20% -> 20%
where the time goes in v3:
time: 114 us
  starting transfers between devices  46.2 us (41%)
  waiting for transfers between devices  39.4 us (35%)
  Pallas kernels  25 us (22%)
  local copies, waits for them, and re-layouts  2.27 us (2%)
    pallas_call x14, Pallas kernels, product(): pl.pallas_call(functools.partial(product_kernel, ring, slot, loads, with_...  19.6 us
    ppermute x6, starting transfers between devices, ring_apply(): came = lax.ppermute(after(first, acc[:1]), AXES, ring.shift())  14.6 us
    ppermute x6, starting transfers between devices, ring_apply(): second = lax.ppermute(after(second, acc[:1]), AXES, ring.shift())  12.4 us
    ppermute x14, waiting for transfers between devices, swap(): lax.ppermute(value, axis, [(i, i ^ distance) for i in range(lax.axis_size...  11.3 us
    ppermute x6, waiting for transfers between devices, ring_apply(): came = lax.ppermute(after(first, acc[:1]), AXES, ring.shift())  8.47 us
    ppermute x4, starting transfers between devices, sum_part(): value += lax.ppermute(value, AXES, [(i, i ^ unit) for i in range(devices)])  7.77 us
    ppermute x14, starting transfers between devices, swap(): lax.ppermute(value, axis, [(i, i ^ distance) for i in range(lax.axis_size...  6.89 us
    ppermute x2, waiting for transfers between devices, ring_apply(): first = lax.ppermute(after(first, acc[:1]), AXES, ring.shift())  6.8 us
  transfers between devices with their start and end apart: 32, of which 21 were waited for; matrix products, arithmetic and copies ran while one was open for 0% of the time, Pallas kernels for 20%

profile of v3, /device:TPU:0, one launch (start us, length us, event | category | flops | bytes accessed | tf_op | source)
XLA Modules:
  0.0 113.8 jit_solution(16205777695547459253)
XLA Ops:
  3.9 2.6 %collective-permute-start = (bf16[1920,128]{1,0:T(8,128)(2,1)S(1)}, bf16[1920,128]{1,0:T(8,128)(2,1)S(1)}, u32[]{:S(2)}, u32[]{:S(2)}) collective-permute-start(bf16[1920,128]{1,0:T(8,128)(2,1)S(1)} %get-tuple-element.76.first), channel_id=1, source_target_pairs={{0,4},{1,2},{4,8},{5,1},{8,12},{9,5},{12,15},{13,9},{15,11},{14,13... | collective-permute-start | bytes 1474568 | tf_op jit(solution)/shard_map/ppermute | solution.py:301
  6.5 3.0 %shard_map.47 = (bf16[1792,7168]{1,0:T(8,128)(2,1)S(1)}, bf16[1792,128]{1,0:T(8,128)(2,1)S(1)}, bf16[1920,128]{1,0:T(8,128)(2,1)S(1)}) custom-call(bf16[1792,7168]{1,0:T(8,128)(2,1)} %refs_2_.3, bf16[128,1792]{1,0:T(8,128)(2,1)S(1)} %get-tuple-element.77.acts.refs_0_, ...), custom_call_target="tpu_custom_call", output_to_operand_aliasing={{2}: (2, {})} | custom-call | tf_op jit(solution)/shard_map/pallas_call | solution.py:165
  13.0 2.4 %collective-permute-start.2 = (bf16[1920,128]{1,0:T(8,128)(2,1)S(1)}, bf16[1920,128]{1,0:T(8,128)(2,1)S(1)}, u32[]{:S(2)}, u32[]{:S(2)}) collective-permute-start(bf16[1920,128]{1,0:T(8,128)(2,1)S(1)} %collective-permute-done.first), channel_id=1, source_target_pairs={{0,4},{1,2},{4,8},{5,1},{8,12},{9,5},{12,15},{13,9},{15,11},{14,13... | collective-permute-start | bytes 1474568 | tf_op jit(solution)/shard_map/ppermute | solution.py:301
  15.3 3.0 %shard_map.48 = (f32[1792,128]{1,0:T(8,128)S(1)}, f32[1792,128]{1,0:T(8,128)S(1)}, bf16[1792,7168]{1,0:T(8,128)(2,1)S(1)}, f32[8,128]{1,0:T(8,128)S(1)}) custom-call(bf16[1920,128]{1,0:T(8,128)(2,1)S(1)} %get-tuple-element.76.first, bf16[1920,128]{1,0:T(8,128)(2,1)S(1)} %get-tuple-element.78.second, ...), custom_call_target="tpu_custom_call", output_to_operand_aliasing={{2}: (5, {})} | custom-call | flops 1644167168 | bytes 6422528 | tf_op jit(solution)/shard_map/pallas_call | solution.py:256
  20.6 2.9 %shard_map.49 = (f32[1792,128]{1,0:T(8,128)S(1)}, f32[1792,128]{1,0:T(8,128)S(1)}, bf16[1792,7168]{1,0:T(8,128)(2,1)S(1)}) custom-call(bf16[1920,128]{1,0:T(8,128)(2,1)S(1)} %collective-permute-done.first, bf16[1920,128]{1,0:T(8,128)(2,1)S(1)} %collective-permute-done.3.second, ...), custom_call_target="tpu_custom_call", output_to_operand_aliasing={{0}: (3, {}), {1}: (4, {}), {2}: (6, {})} | custom-call | flops 1644167168 | bytes 6422528 | tf_op jit(solution)/shard_map/pallas_call | solution.py:256
  23.6 2.3 %collective-permute-start.4 = (bf16[1920,128]{1,0:T(8,128)(2,1)S(1)}, bf16[1920,128]{1,0:T(8,128)(2,1)S(1)}, u32[]{:S(2)}, u32[]{:S(2)}) collective-permute-start(bf16[1920,128]{1,0:T(8,128)(2,1)S(1)} %collective-permute-done.2.first), channel_id=1, source_target_pairs={{0,4},{1,2},{4,8},{5,1},{8,12},{9,5},{12,15},{13,9},{15,11},{14,13... | collective-permute-start | bytes 1474568 | tf_op jit(solution)/shard_map/ppermute | solution.py:301
  25.9 2.9 %shard_map.50 = (f32[1792,128]{1,0:T(8,128)S(1)}, f32[1792,128]{1,0:T(8,128)S(1)}, bf16[1792,7168]{1,0:T(8,128)(2,1)S(1)}) custom-call(bf16[1920,128]{1,0:T(8,128)(2,1)S(1)} %collective-permute-done.6.first, bf16[1920,128]{1,0:T(8,128)(2,1)S(1)} %collective-permute-done.7.second, ...), custom_call_target="tpu_custom_call", output_to_operand_aliasing={{0}: (3, {}), {1}: (4, {}), {2}: (6, {})} | custom-call | flops 493250144 | bytes 1926758 | tf_op jit(solution)/shard_map/pallas_call | solution.py:256
  28.8 2.3 %collective-permute-start.10 = (bf16[1920,128]{1,0:T(8,128)(2,1)S(1)}, bf16[1920,128]{1,0:T(8,128)(2,1)S(1)}, u32[]{:S(2)}, u32[]{:S(2)}) collective-permute-start(bf16[1920,128]{1,0:T(8,128)(2,1)S(1)} %collective-permute-done.5.second), channel_id=1, source_target_pairs={{0,4},{1,2},{4,8},{5,1},{8,12},{9,5},{12,15},{13,9},{15,11},{14,13... | collective-permute-start | bytes 1474568 | tf_op jit(solution)/shard_map/ppermute | solution.py:304
  36.4 2.9 %collective-permute-done.10.second = bf16[1920,128]{1,0:T(8,128)(2,1)S(1)} collective-permute-done((bf16[1920,128]{1,0:T(8,128)(2,1)S(1)}, bf16[1920,128]{1,0:T(8,128)(2,1)S(1)}, u32[]{:S(2)}, u32[]{:S(2)}) %collective-permute-start.10) | collective-permute-done | bytes 491552 | tf_op jit(solution)/shard_map/ppermute | solution.py:304
  41.2 3.4 %collective-permute-done.8.first = bf16[1920,128]{1,0:T(8,128)(2,1)S(1)} collective-permute-done((bf16[1920,128]{1,0:T(8,128)(2,1)S(1)}, bf16[1920,128]{1,0:T(8,128)(2,1)S(1)}, u32[]{:S(2)}, u32[]{:S(2)}) %collective-permute-start.8) | collective-permute-done | bytes 491552 | tf_op jit(solution)/shard_map/ppermute | solution.py:311
  46.5 2.3 %collective-permute-start.13 = (f32[1792,128]{1,0:T(8,128)S(1)}, f32[1792,128]{1,0:T(8,128)S(1)}, u32[]{:S(2)}, u32[]{:S(2)}) collective-permute-start(f32[1792,128]{1,0:T(8,128)S(1)} %get-tuple-element.109), channel_id=1, source_target_pairs={{0,1},{1,0},{2,3},{3,2},{4,5},{5,4},{6,7},{7,6},{8,9},{9,8},{10,11... | collective-permute-start | bytes 2752520 | tf_op jit(solution)/shard_map/ppermute | solution.py:22
  51.7 2.3 %collective-permute-start.14 = (bf16[1920,128]{1,0:T(8,128)(2,1)S(1)}, bf16[1920,128]{1,0:T(8,128)(2,1)S(1)}, u32[]{:S(2)}, u32[]{:S(2)}) collective-permute-start(bf16[1920,128]{1,0:T(8,128)(2,1)S(1)} %get-tuple-element.113.first), channel_id=1, source_target_pairs={{0,4},{1,2},{4,8},{5,1},{8,12},{9,5},{12,15},{13,9},{15,11},{14,13... | collective-permute-start | bytes 1474568 | tf_op jit(solution)/shard_map/ppermute | solution.py:301
  55.7 4.7 %collective-permute-done.14.first = bf16[1920,128]{1,0:T(8,128)(2,1)S(1)} collective-permute-done((bf16[1920,128]{1,0:T(8,128)(2,1)S(1)}, bf16[1920,128]{1,0:T(8,128)(2,1)S(1)}, u32[]{:S(2)}, u32[]{:S(2)}) %collective-permute-start.14) | collective-permute-done | bytes 491552 | tf_op jit(solution)/shard_map/ppermute | solution.py:301
  60.4 2.5 %collective-permute-start.15 = (bf16[1920,128]{1,0:T(8,128)(2,1)S(1)}, bf16[1920,128]{1,0:T(8,128)(2,1)S(1)}, u32[]{:S(2)}, u32[]{:S(2)}) collective-permute-start(bf16[1920,128]{1,0:T(8,128)(2,1)S(1)} %collective-permute-done.14.first), channel_id=1, source_target_pairs={{0,4},{1,2},{4,8},{5,1},{8,12},{9,5},{12,15},{13,9},{15,11},{14,13... | collective-permute-start | bytes 1474568 | tf_op jit(solution)/shard_map/ppermute | solution.py:301
  62.9 2.3 %shard_map.56 = (f32[1792,128]{1,0:T(8,128)S(1)}, f32[1792,128]{1,0:T(8,128)S(1)}, bf16[1792,7168]{1,0:T(8,128)(2,1)S(1)}) custom-call(bf16[1920,128]{1,0:T(8,128)(2,1)S(1)} %get-tuple-element.113.first, bf16[1920,128]{1,0:T(8,128)(2,1)S(1)} %collective-permute-done.16.second, ...), custom_call_target="tpu_custom_call", output_to_operand_aliasing={{2}: (3, {})} | custom-call | flops 1644167168 | bytes 6422528 | tf_op jit(solution)/shard_map/pallas_call | solution.py:256
  65.7 2.4 %collective-permute-start.19 = (bf16[1920,128]{1,0:T(8,128)(2,1)S(1)}, bf16[1920,128]{1,0:T(8,128)(2,1)S(1)}, u32[]{:S(2)}, u32[]{:S(2)}) collective-permute-start(bf16[1920,128]{1,0:T(8,128)(2,1)S(1)} %collective-permute-done.17.second), channel_id=1, source_target_pairs={{0,4},{1,2},{4,8},{5,1},{8,12},{9,5},{12,15},{13,9},{15,11},{14,13... | collective-permute-start | bytes 1474568 | tf_op jit(solution)/shard_map/ppermute | solution.py:304
  70.9 2.5 %collective-permute-start.18 = (bf16[1920,128]{1,0:T(8,128)(2,1)S(1)}, bf16[1920,128]{1,0:T(8,128)(2,1)S(1)}, u32[]{:S(2)}, u32[]{:S(2)}) collective-permute-start(bf16[1920,128]{1,0:T(8,128)(2,1)S(1)} %collective-permute-done.15.first), channel_id=1, source_target_pairs={{0,4},{1,2},{4,8},{5,1},{8,12},{9,5},{12,15},{13,9},{15,11},{14,13... | collective-permute-start | bytes 1474568 | tf_op jit(solution)/shard_map/ppermute | solution.py:301
  76.2 2.5 %collective-permute-start.24 = (bf16[1920,128]{1,0:T(8,128)(2,1)S(1)}, bf16[1920,128]{1,0:T(8,128)(2,1)S(1)}, u32[]{:S(2)}, u32[]{:S(2)}) collective-permute-start(bf16[1920,128]{1,0:T(8,128)(2,1)S(1)} %collective-permute-done.19.second), channel_id=1, source_target_pairs={{0,4},{1,2},{4,8},{5,1},{8,12},{9,5},{12,15},{13,9},{15,11},{14,13... | collective-permute-start | bytes 1474568 | tf_op jit(solution)/shard_map/ppermute | solution.py:304
  81.5 2.5 %collective-permute-start.22 = (bf16[1920,128]{1,0:T(8,128)(2,1)S(1)}, bf16[1920,128]{1,0:T(8,128)(2,1)S(1)}, u32[]{:S(2)}, u32[]{:S(2)}) collective-permute-start(bf16[1920,128]{1,0:T(8,128)(2,1)S(1)} %collective-permute-done.18.first), channel_id=1, source_target_pairs={{0,4},{1,2},{4,8},{5,1},{8,12},{9,5},{12,15},{13,9},{15,11},{14,13... | collective-permute-start | bytes 1474568 | tf_op jit(solution)/shard_map/ppermute | solution.py:311
  83.9 2.8 %collective-permute-done.24.second = bf16[1920,128]{1,0:T(8,128)(2,1)S(1)} collective-permute-done((bf16[1920,128]{1,0:T(8,128)(2,1)S(1)}, bf16[1920,128]{1,0:T(8,128)(2,1)S(1)}, u32[]{:S(2)}, u32[]{:S(2)}) %collective-permute-start.24) | collective-permute-done | bytes 491552 | tf_op jit(solution)/shard_map/ppermute | solution.py:304
  88.6 3.4 %collective-permute-done.22.first = bf16[1920,128]{1,0:T(8,128)(2,1)S(1)} collective-permute-done((bf16[1920,128]{1,0:T(8,128)(2,1)S(1)}, bf16[1920,128]{1,0:T(8,128)(2,1)S(1)}, u32[]{:S(2)}, u32[]{:S(2)}) %collective-permute-start.22) | collective-permute-done | bytes 491552 | tf_op jit(solution)/shard_map/ppermute | solution.py:311
  93.9 2.3 %collective-permute-start.27 = (f32[1792,128]{1,0:T(8,128)S(1)}, f32[1792,128]{1,0:T(8,128)S(1)}, u32[]{:S(2)}, u32[]{:S(2)}) collective-permute-start(f32[1792,128]{1,0:T(8,128)S(1)} %get-tuple-element.142), channel_id=1, source_target_pairs={{0,1},{1,0},{2,3},{3,2},{4,5},{5,4},{6,7},{7,6},{8,9},{9,8},{10,11... | collective-permute-start | bytes 2752520 | tf_op jit(solution)/shard_map/ppermute | solution.py:22
  103.5 2.4 %collective-permute-start.30 = (f32[8,128]{1,0:T(8,128)S(1)}, f32[8,128]{1,0:T(8,128)S(1)}, u32[]{:S(2)}, u32[]{:S(2)}) collective-permute-start(f32[8,128]{1,0:T(8,128)S(1)} %add.21), channel_id=1, source_target_pairs={{0,4},{1,5},{2,6},{3,7},{4,0},{5,1},{6,2},{7,3},{8,12},{9,13},{10,... | collective-permute-start | bytes 12296 | tf_op jit(solution)/shard_map/ppermute | solution.py:29
  107.5 3.4 %collective-permute-start.31 = (f32[8,128]{1,0:T(8,128)S(1)}, f32[8,128]{1,0:T(8,128)S(1)}, u32[]{:S(2)}, u32[]{:S(2)}) collective-permute-start(f32[8,128]{1,0:T(8,128)S(1)} %add.22), channel_id=1, source_target_pairs={{0,8},{1,9},{2,10},{3,11},{4,12},{5,13},{6,14},{7,15},{8,0},{9,1},... | collective-permute-start | bytes 12296 | tf_op jit(solution)/shard_map/ppermute | solution.py:29
  (71 shorter events, 47.6 us)
Async XLA Ops:
  3.9 9.1 %collective-permute-start = (bf16[1920,128]{1,0:T(8,128)(2,1)S(1)}, bf16[1920,128]{1,0:T(8,128)(2,1)S(1)}, u32[]{:S(2)}, u32[]{:S(2)}) collective-permute-start(bf16[1920,128]{1,0:T(8,128)(2,1)S(1)} %get-tuple-element.76.first), channel_id=1, source_target_pairs={{0,4},{1,2},{4,8},{5,1},{8,12},{9,5},{12,15},{13,9},{15,11},{14,13... | collective-permute-start | bytes 1474568 | tf_op jit(solution)/shard_map/ppermute | solution.py:301
  9.5 9.0 %collective-permute-start.3 = (bf16[1920,128]{1,0:T(8,128)(2,1)S(1)}, bf16[1920,128]{1,0:T(8,128)(2,1)S(1)}, u32[]{:S(2)}, u32[]{:S(2)}) collective-permute-start(bf16[1920,128]{1,0:T(8,128)(2,1)S(1)} %get-tuple-element.78.second), channel_id=1, source_target_pairs={{0,4},{1,2},{4,8},{5,1},{8,12},{9,5},{12,15},{13,9},{15,11},{14,13... | collective-permute-start | bytes 1474568 | tf_op jit(solution)/shard_map/ppermute | solution.py:304
  13.0 10.6 %collective-permute-start.2 = (bf16[1920,128]{1,0:T(8,128)(2,1)S(1)}, bf16[1920,128]{1,0:T(8,128)(2,1)S(1)}, u32[]{:S(2)}, u32[]{:S(2)}) collective-permute-start(bf16[1920,128]{1,0:T(8,128)(2,1)S(1)} %collective-permute-done.first), channel_id=1, source_target_pairs={{0,4},{1,2},{4,8},{5,1},{8,12},{9,5},{12,15},{13,9},{15,11},{14,13... | collective-permute-start | bytes 1474568 | tf_op jit(solution)/shard_map/ppermute | solution.py:301
  18.4 5.2 %collective-permute-start.6 = (bf16[1920,128]{1,0:T(8,128)(2,1)S(1)}, bf16[1920,128]{1,0:T(8,128)(2,1)S(1)}, u32[]{:S(2)}, u32[]{:S(2)}) collective-permute-start(bf16[1920,128]{1,0:T(8,128)(2,1)S(1)} %collective-permute-done.first), channel_id=1, source_target_pairs={{0,1},{1,0},{2,3},{3,2},{4,5},{5,4},{6,7},{7,6},{8,9},{9,8},{10,11... | collective-permute-start | bytes 1474568 | tf_op jit(solution)/shard_map/ppermute | solution.py:22
  18.5 7.4 %collective-permute-start.7 = (bf16[1920,128]{1,0:T(8,128)(2,1)S(1)}, bf16[1920,128]{1,0:T(8,128)(2,1)S(1)}, u32[]{:S(2)}, u32[]{:S(2)}) collective-permute-start(bf16[1920,128]{1,0:T(8,128)(2,1)S(1)} %collective-permute-done.3.second), channel_id=1, source_target_pairs={{0,1},{1,0},{2,3},{3,2},{4,5},{5,4},{6,7},{7,6},{8,9},{9,8},{10,11... | collective-permute-start | bytes 1474568 | tf_op jit(solution)/shard_map/ppermute | solution.py:22
  19.0 9.8 %collective-permute-start.5 = (bf16[1920,128]{1,0:T(8,128)(2,1)S(1)}, bf16[1920,128]{1,0:T(8,128)(2,1)S(1)}, u32[]{:S(2)}, u32[]{:S(2)}) collective-permute-start(bf16[1920,128]{1,0:T(8,128)(2,1)S(1)} %collective-permute-done.3.second), channel_id=1, source_target_pairs={{0,4},{1,2},{4,8},{5,1},{8,12},{9,5},{12,15},{13,9},{15,11},{14,13... | collective-permute-start | bytes 1474568 | tf_op jit(solution)/shard_map/ppermute | solution.py:304
  23.6 10.5 %collective-permute-start.4 = (bf16[1920,128]{1,0:T(8,128)(2,1)S(1)}, bf16[1920,128]{1,0:T(8,128)(2,1)S(1)}, u32[]{:S(2)}, u32[]{:S(2)}) collective-permute-start(bf16[1920,128]{1,0:T(8,128)(2,1)S(1)} %collective-permute-done.2.first), channel_id=1, source_target_pairs={{0,4},{1,2},{4,8},{5,1},{8,12},{9,5},{12,15},{13,9},{15,11},{14,13... | collective-permute-start | bytes 1474568 | tf_op jit(solution)/shard_map/ppermute | solution.py:301
  28.8 10.5 %collective-permute-start.10 = (bf16[1920,128]{1,0:T(8,128)(2,1)S(1)}, bf16[1920,128]{1,0:T(8,128)(2,1)S(1)}, u32[]{:S(2)}, u32[]{:S(2)}) collective-permute-start(bf16[1920,128]{1,0:T(8,128)(2,1)S(1)} %collective-permute-done.5.second), channel_id=1, source_target_pairs={{0,4},{1,2},{4,8},{5,1},{8,12},{9,5},{12,15},{13,9},{15,11},{14,13... | collective-permute-start | bytes 1474568 | tf_op jit(solution)/shard_map/ppermute | solution.py:304
  34.1 5.5 %collective-permute-start.9 = (bf16[1920,128]{1,0:T(8,128)(2,1)S(1)}, bf16[1920,128]{1,0:T(8,128)(2,1)S(1)}, u32[]{:S(2)}, u32[]{:S(2)}) collective-permute-start(bf16[1920,128]{1,0:T(8,128)(2,1)S(1)} %collective-permute-done.4.first), channel_id=1, source_target_pairs={{0,1},{1,0},{2,3},{3,2},{4,5},{5,4},{6,7},{7,6},{8,9},{9,8},{10,11... | collective-permute-start | bytes 1474568 | tf_op jit(solution)/shard_map/ppermute | solution.py:22
  34.3 10.3 %collective-permute-start.8 = (bf16[1920,128]{1,0:T(8,128)(2,1)S(1)}, bf16[1920,128]{1,0:T(8,128)(2,1)S(1)}, u32[]{:S(2)}, u32[]{:S(2)}) collective-permute-start(bf16[1920,128]{1,0:T(8,128)(2,1)S(1)} %collective-permute-done.4.first), channel_id=1, source_target_pairs={{0,4},{1,2},{4,8},{5,1},{8,12},{9,5},{12,15},{13,9},{15,11},{14,13... | collective-permute-start | bytes 1474568 | tf_op jit(solution)/shard_map/ppermute | solution.py:311
  46.5 4.4 %collective-permute-start.13 = (f32[1792,128]{1,0:T(8,128)S(1)}, f32[1792,128]{1,0:T(8,128)S(1)}, u32[]{:S(2)}, u32[]{:S(2)}) collective-permute-start(f32[1792,128]{1,0:T(8,128)S(1)} %get-tuple-element.109), channel_id=1, source_target_pairs={{0,1},{1,0},{2,3},{3,2},{4,5},{5,4},{6,7},{7,6},{8,9},{9,8},{10,11... | collective-permute-start | bytes 2752520 | tf_op jit(solution)/shard_map/ppermute | solution.py:22
  51.7 8.6 %collective-permute-start.14 = (bf16[1920,128]{1,0:T(8,128)(2,1)S(1)}, bf16[1920,128]{1,0:T(8,128)(2,1)S(1)}, u32[]{:S(2)}, u32[]{:S(2)}) collective-permute-start(bf16[1920,128]{1,0:T(8,128)(2,1)S(1)} %get-tuple-element.113.first), channel_id=1, source_target_pairs={{0,4},{1,2},{4,8},{5,1},{8,12},{9,5},{12,15},{13,9},{15,11},{14,13... | collective-permute-start | bytes 1474568 | tf_op jit(solution)/shard_map/ppermute | solution.py:301
  54.0 11.6 %collective-permute-start.17 = (bf16[1920,128]{1,0:T(8,128)(2,1)S(1)}, bf16[1920,128]{1,0:T(8,128)(2,1)S(1)}, u32[]{:S(2)}, u32[]{:S(2)}) collective-permute-start(bf16[1920,128]{1,0:T(8,128)(2,1)S(1)} %collective-permute-done.16.second), channel_id=1, source_target_pairs={{0,4},{1,2},{4,8},{5,1},{8,12},{9,5},{12,15},{13,9},{15,11},{14,13... | collective-permute-start | bytes 1474568 | tf_op jit(solution)/shard_map/ppermute | solution.py:304
  60.4 10.5 %collective-permute-start.15 = (bf16[1920,128]{1,0:T(8,128)(2,1)S(1)}, bf16[1920,128]{1,0:T(8,128)(2,1)S(1)}, u32[]{:S(2)}, u32[]{:S(2)}) collective-permute-start(bf16[1920,128]{1,0:T(8,128)(2,1)S(1)} %collective-permute-done.14.first), channel_id=1, source_target_pairs={{0,4},{1,2},{4,8},{5,1},{8,12},{9,5},{12,15},{13,9},{15,11},{14,13... | collective-permute-start | bytes 1474568 | tf_op jit(solution)/shard_map/ppermute | solution.py:301
  65.1 8.3 %collective-permute-start.20 = (bf16[1920,128]{1,0:T(8,128)(2,1)S(1)}, bf16[1920,128]{1,0:T(8,128)(2,1)S(1)}, u32[]{:S(2)}, u32[]{:S(2)}) collective-permute-start(bf16[1920,128]{1,0:T(8,128)(2,1)S(1)} %collective-permute-done.14.first), channel_id=1, source_target_pairs={{0,1},{1,0},{2,3},{3,2},{4,5},{5,4},{6,7},{7,6},{8,9},{9,8},{10,11... | collective-permute-start | bytes 1474568 | tf_op jit(solution)/shard_map/ppermute | solution.py:22
  65.7 7.8 %collective-permute-start.21 = (bf16[1920,128]{1,0:T(8,128)(2,1)S(1)}, bf16[1920,128]{1,0:T(8,128)(2,1)S(1)}, u32[]{:S(2)}, u32[]{:S(2)}) collective-permute-start(bf16[1920,128]{1,0:T(8,128)(2,1)S(1)} %collective-permute-done.17.second), channel_id=1, source_target_pairs={{0,1},{1,0},{2,3},{3,2},{4,5},{5,4},{6,7},{7,6},{8,9},{9,8},{10,11... | collective-permute-start | bytes 1474568 | tf_op jit(solution)/shard_map/ppermute | solution.py:22
  65.7 10.5 %collective-permute-start.19 = (bf16[1920,128]{1,0:T(8,128)(2,1)S(1)}, bf16[1920,128]{1,0:T(8,128)(2,1)S(1)}, u32[]{:S(2)}, u32[]{:S(2)}) collective-permute-start(bf16[1920,128]{1,0:T(8,128)(2,1)S(1)} %collective-permute-done.17.second), channel_id=1, source_target_pairs={{0,4},{1,2},{4,8},{5,1},{8,12},{9,5},{12,15},{13,9},{15,11},{14,13... | collective-permute-start | bytes 1474568 | tf_op jit(solution)/shard_map/ppermute | solution.py:304
  70.9 10.5 %collective-permute-start.18 = (bf16[1920,128]{1,0:T(8,128)(2,1)S(1)}, bf16[1920,128]{1,0:T(8,128)(2,1)S(1)}, u32[]{:S(2)}, u32[]{:S(2)}) collective-permute-start(bf16[1920,128]{1,0:T(8,128)(2,1)S(1)} %collective-permute-done.15.first), channel_id=1, source_target_pairs={{0,4},{1,2},{4,8},{5,1},{8,12},{9,5},{12,15},{13,9},{15,11},{14,13... | collective-permute-start | bytes 1474568 | tf_op jit(solution)/shard_map/ppermute | solution.py:301
  76.2 10.5 %collective-permute-start.24 = (bf16[1920,128]{1,0:T(8,128)(2,1)S(1)}, bf16[1920,128]{1,0:T(8,128)(2,1)S(1)}, u32[]{:S(2)}, u32[]{:S(2)}) collective-permute-start(bf16[1920,128]{1,0:T(8,128)(2,1)S(1)} %collective-permute-done.19.second), channel_id=1, source_target_pairs={{0,4},{1,2},{4,8},{5,1},{8,12},{9,5},{12,15},{13,9},{15,11},{14,13... | collective-permute-start | bytes 1474568 | tf_op jit(solution)/shard_map/ppermute | solution.py:304
  81.5 5.3 %collective-permute-start.23 = (bf16[1920,128]{1,0:T(8,128)(2,1)S(1)}, bf16[1920,128]{1,0:T(8,128)(2,1)S(1)}, u32[]{:S(2)}, u32[]{:S(2)}) collective-permute-start(bf16[1920,128]{1,0:T(8,128)(2,1)S(1)} %collective-permute-done.18.first), channel_id=1, source_target_pairs={{0,1},{1,0},{2,3},{3,2},{4,5},{5,4},{6,7},{7,6},{8,9},{9,8},{10,11... | collective-permute-start | bytes 1474568 | tf_op jit(solution)/shard_map/ppermute | solution.py:22
  81.5 10.5 %collective-permute-start.22 = (bf16[1920,128]{1,0:T(8,128)(2,1)S(1)}, bf16[1920,128]{1,0:T(8,128)(2,1)S(1)}, u32[]{:S(2)}, u32[]{:S(2)}) collective-permute-start(bf16[1920,128]{1,0:T(8,128)(2,1)S(1)} %collective-permute-done.18.first), channel_id=1, source_target_pairs={{0,4},{1,2},{4,8},{5,1},{8,12},{9,5},{12,15},{13,9},{15,11},{14,13... | collective-permute-start | bytes 1474568 | tf_op jit(solution)/shard_map/ppermute | solution.py:311
  93.9 4.4 %collective-permute-start.27 = (f32[1792,128]{1,0:T(8,128)S(1)}, f32[1792,128]{1,0:T(8,128)S(1)}, u32[]{:S(2)}, u32[]{:S(2)}) collective-permute-start(f32[1792,128]{1,0:T(8,128)S(1)} %get-tuple-element.142), channel_id=1, source_target_pairs={{0,1},{1,0},{2,3},{3,2},{4,5},{5,4},{6,7},{7,6},{8,9},{9,8},{10,11... | collective-permute-start | bytes 2752520 | tf_op jit(solution)/shard_map/ppermute | solution.py:22
  103.5 4.0 %collective-permute-start.30 = (f32[8,128]{1,0:T(8,128)S(1)}, f32[8,128]{1,0:T(8,128)S(1)}, u32[]{:S(2)}, u32[]{:S(2)}) collective-permute-start(f32[8,128]{1,0:T(8,128)S(1)} %add.21), channel_id=1, source_target_pairs={{0,4},{1,5},{2,6},{3,7},{4,0},{5,1},{6,2},{7,3},{8,12},{9,13},{10,... | collective-permute-start | bytes 12296 | tf_op jit(solution)/shard_map/ppermute | solution.py:29
  107.5 5.0 %collective-permute-start.31 = (f32[8,128]{1,0:T(8,128)S(1)}, f32[8,128]{1,0:T(8,128)S(1)}, u32[]{:S(2)}, u32[]{:S(2)}) collective-permute-start(f32[8,128]{1,0:T(8,128)S(1)} %add.22), channel_id=1, source_target_pairs={{0,8},{1,9},{2,10},{3,11},{4,12},{5,13},{6,14},{7,15},{8,0},{9,1},... | collective-permute-start | bytes 12296 | tf_op jit(solution)/shard_map/ppermute | solution.py:29
  (11 other events, 44.3 us)

commit v4 on v3

--- a/solution.py
+++ b/solution.py
@@ -24,10 +24,10 @@
 
 def sum_part(value, count):
     devices = 2 * count
-    unit = 1
-    while unit < devices:
+    unit = devices // 2
+    while unit:
         value += lax.ppermute(value, AXES, [(i, i ^ unit) for i in range(devices)])
-        unit *= 2
+        unit //= 2
     return value
 
 

time: 114 us -> 114 us (level)
  no operation moved by 1% of the time
where the time goes in v4:
time: 114 us
  starting transfers between devices  45.3 us (40%)
  waiting for transfers between devices  40.3 us (35%)
  Pallas kernels  25 us (22%)
  local copies, waits for them, and re-layouts  2.27 us (2%)
    pallas_call x14, Pallas kernels, product(): pl.pallas_call(functools.partial(product_kernel, ring, slot, loads, with_...  19.6 us
    ppermute x6, starting transfers between devices, ring_apply(): came = lax.ppermute(after(first, acc[:1]), AXES, ring.shift())  14.6 us
    ppermute x6, starting transfers between devices, ring_apply(): second = lax.ppermute(after(second, acc[:1]), AXES, ring.shift())  12.4 us
    ppermute x14, waiting for transfers between devices, swap(): lax.ppermute(value, axis, [(i, i ^ distance) for i in range(lax.axis_size...  11.3 us
    ppermute x6, waiting for transfers between devices, ring_apply(): came = lax.ppermute(after(first, acc[:1]), AXES, ring.shift())  8.47 us
    ppermute x4, waiting for transfers between devices, sum_part(): value += lax.ppermute(value, AXES, [(i, i ^ unit) for i in range(devices)])  6.95 us
    ppermute x14, starting transfers between devices, swap(): lax.ppermute(value, axis, [(i, i ^ distance) for i in range(lax.axis_size...  6.89 us
    ppermute x4, starting transfers between devices, sum_part(): value += lax.ppermute(value, AXES, [(i, i ^ unit) for i in range(devices)])  6.87 us
  transfers between devices with their start and end apart: 32, of which 21 were waited for; matrix products, arithmetic and copies ran while one was open for 0% of the time, Pallas kernels for 20%

profile of v4, /device:TPU:0, one launch (start us, length us, event | category | flops | bytes accessed | tf_op | source)
XLA Modules:
  0.0 113.8 jit_solution(7063792923705309738)
XLA Ops:
  3.9 2.6 %collective-permute-start = (bf16[1920,128]{1,0:T(8,128)(2,1)S(1)}, bf16[1920,128]{1,0:T(8,128)(2,1)S(1)}, u32[]{:S(2)}, u32[]{:S(2)}) collective-permute-start(bf16[1920,128]{1,0:T(8,128)(2,1)S(1)} %get-tuple-element.76.first), channel_id=1, source_target_pairs={{0,4},{1,2},{4,8},{5,1},{8,12},{9,5},{12,15},{13,9},{15,11},{14,13... | collective-permute-start | bytes 1474568 | tf_op jit(solution)/shard_map/ppermute | solution.py:301
  6.5 3.0 %shard_map.47 = (bf16[1792,7168]{1,0:T(8,128)(2,1)S(1)}, bf16[1792,128]{1,0:T(8,128)(2,1)S(1)}, bf16[1920,128]{1,0:T(8,128)(2,1)S(1)}) custom-call(bf16[1792,7168]{1,0:T(8,128)(2,1)} %refs_2_.3, bf16[128,1792]{1,0:T(8,128)(2,1)S(1)} %get-tuple-element.77.acts.refs_0_, ...), custom_call_target="tpu_custom_call", output_to_operand_aliasing={{2}: (2, {})} | custom-call | tf_op jit(solution)/shard_map/pallas_call | solution.py:165
  13.0 2.4 %collective-permute-start.2 = (bf16[1920,128]{1,0:T(8,128)(2,1)S(1)}, bf16[1920,128]{1,0:T(8,128)(2,1)S(1)}, u32[]{:S(2)}, u32[]{:S(2)}) collective-permute-start(bf16[1920,128]{1,0:T(8,128)(2,1)S(1)} %collective-permute-done.first), channel_id=1, source_target_pairs={{0,4},{1,2},{4,8},{5,1},{8,12},{9,5},{12,15},{13,9},{15,11},{14,13... | collective-permute-start | bytes 1474568 | tf_op jit(solution)/shard_map/ppermute | solution.py:301
  15.3 3.0 %shard_map.48 = (f32[1792,128]{1,0:T(8,128)S(1)}, f32[1792,128]{1,0:T(8,128)S(1)}, bf16[1792,7168]{1,0:T(8,128)(2,1)S(1)}, f32[8,128]{1,0:T(8,128)S(1)}) custom-call(bf16[1920,128]{1,0:T(8,128)(2,1)S(1)} %get-tuple-element.76.first, bf16[1920,128]{1,0:T(8,128)(2,1)S(1)} %get-tuple-element.78.second, ...), custom_call_target="tpu_custom_call", output_to_operand_aliasing={{2}: (5, {})} | custom-call | flops 1644167168 | bytes 6422528 | tf_op jit(solution)/shard_map/pallas_call | solution.py:256
  20.6 2.9 %shard_map.49 = (f32[1792,128]{1,0:T(8,128)S(1)}, f32[1792,128]{1,0:T(8,128)S(1)}, bf16[1792,7168]{1,0:T(8,128)(2,1)S(1)}) custom-call(bf16[1920,128]{1,0:T(8,128)(2,1)S(1)} %collective-permute-done.first, bf16[1920,128]{1,0:T(8,128)(2,1)S(1)} %collective-permute-done.3.second, ...), custom_call_target="tpu_custom_call", output_to_operand_aliasing={{0}: (3, {}), {1}: (4, {}), {2}: (6, {})} | custom-call | flops 1644167168 | bytes 6422528 | tf_op jit(solution)/shard_map/pallas_call | solution.py:256
  23.6 2.3 %collective-permute-start.4 = (bf16[1920,128]{1,0:T(8,128)(2,1)S(1)}, bf16[1920,128]{1,0:T(8,128)(2,1)S(1)}, u32[]{:S(2)}, u32[]{:S(2)}) collective-permute-start(bf16[1920,128]{1,0:T(8,128)(2,1)S(1)} %collective-permute-done.2.first), channel_id=1, source_target_pairs={{0,4},{1,2},{4,8},{5,1},{8,12},{9,5},{12,15},{13,9},{15,11},{14,13... | collective-permute-start | bytes 1474568 | tf_op jit(solution)/shard_map/ppermute | solution.py:301
  25.9 2.9 %shard_map.50 = (f32[1792,128]{1,0:T(8,128)S(1)}, f32[1792,128]{1,0:T(8,128)S(1)}, bf16[1792,7168]{1,0:T(8,128)(2,1)S(1)}) custom-call(bf16[1920,128]{1,0:T(8,128)(2,1)S(1)} %collective-permute-done.6.first, bf16[1920,128]{1,0:T(8,128)(2,1)S(1)} %collective-permute-done.7.second, ...), custom_call_target="tpu_custom_call", output_to_operand_aliasing={{0}: (3, {}), {1}: (4, {}), {2}: (6, {})} | custom-call | flops 493250144 | bytes 1926758 | tf_op jit(solution)/shard_map/pallas_call | solution.py:256
  28.8 2.3 %collective-permute-start.10 = (bf16[1920,128]{1,0:T(8,128)(2,1)S(1)}, bf16[1920,128]{1,0:T(8,128)(2,1)S(1)}, u32[]{:S(2)}, u32[]{:S(2)}) collective-permute-start(bf16[1920,128]{1,0:T(8,128)(2,1)S(1)} %collective-permute-done.5.second), channel_id=1, source_target_pairs={{0,4},{1,2},{4,8},{5,1},{8,12},{9,5},{12,15},{13,9},{15,11},{14,13... | collective-permute-start | bytes 1474568 | tf_op jit(solution)/shard_map/ppermute | solution.py:304
  34.3 2.2 %collective-permute-start.8 = (bf16[1920,128]{1,0:T(8,128)(2,1)S(1)}, bf16[1920,128]{1,0:T(8,128)(2,1)S(1)}, u32[]{:S(2)}, u32[]{:S(2)}) collective-permute-start(bf16[1920,128]{1,0:T(8,128)(2,1)S(1)} %collective-permute-done.4.first), channel_id=1, source_target_pairs={{0,4},{1,2},{4,8},{5,1},{8,12},{9,5},{12,15},{13,9},{15,11},{14,13... | collective-permute-start | bytes 1474568 | tf_op jit(solution)/shard_map/ppermute | solution.py:311
  36.4 2.9 %collective-permute-done.10.second = bf16[1920,128]{1,0:T(8,128)(2,1)S(1)} collective-permute-done((bf16[1920,128]{1,0:T(8,128)(2,1)S(1)}, bf16[1920,128]{1,0:T(8,128)(2,1)S(1)}, u32[]{:S(2)}, u32[]{:S(2)}) %collective-permute-start.10) | collective-permute-done | bytes 491552 | tf_op jit(solution)/shard_map/ppermute | solution.py:304
  41.2 3.4 %collective-permute-done.8.first = bf16[1920,128]{1,0:T(8,128)(2,1)S(1)} collective-permute-done((bf16[1920,128]{1,0:T(8,128)(2,1)S(1)}, bf16[1920,128]{1,0:T(8,128)(2,1)S(1)}, u32[]{:S(2)}, u32[]{:S(2)}) %collective-permute-start.8) | collective-permute-done | bytes 491552 | tf_op jit(solution)/shard_map/ppermute | solution.py:311
  46.5 2.3 %collective-permute-start.13 = (f32[1792,128]{1,0:T(8,128)S(1)}, f32[1792,128]{1,0:T(8,128)S(1)}, u32[]{:S(2)}, u32[]{:S(2)}) collective-permute-start(f32[1792,128]{1,0:T(8,128)S(1)} %get-tuple-element.109), channel_id=1, source_target_pairs={{0,1},{1,0},{2,3},{3,2},{4,5},{5,4},{6,7},{7,6},{8,9},{9,8},{10,11... | collective-permute-start | bytes 2752520 | tf_op jit(solution)/shard_map/ppermute | solution.py:22
  51.7 2.3 %collective-permute-start.14 = (bf16[1920,128]{1,0:T(8,128)(2,1)S(1)}, bf16[1920,128]{1,0:T(8,128)(2,1)S(1)}, u32[]{:S(2)}, u32[]{:S(2)}) collective-permute-start(bf16[1920,128]{1,0:T(8,128)(2,1)S(1)} %get-tuple-element.113.first), channel_id=1, source_target_pairs={{0,4},{1,2},{4,8},{5,1},{8,12},{9,5},{12,15},{13,9},{15,11},{14,13... | collective-permute-start | bytes 1474568 | tf_op jit(solution)/shard_map/ppermute | solution.py:301
  55.7 4.7 %collective-permute-done.14.first = bf16[1920,128]{1,0:T(8,128)(2,1)S(1)} collective-permute-done((bf16[1920,128]{1,0:T(8,128)(2,1)S(1)}, bf16[1920,128]{1,0:T(8,128)(2,1)S(1)}, u32[]{:S(2)}, u32[]{:S(2)}) %collective-permute-start.14) | collective-permute-done | bytes 491552 | tf_op jit(solution)/shard_map/ppermute | solution.py:301
  60.4 2.5 %collective-permute-start.15 = (bf16[1920,128]{1,0:T(8,128)(2,1)S(1)}, bf16[1920,128]{1,0:T(8,128)(2,1)S(1)}, u32[]{:S(2)}, u32[]{:S(2)}) collective-permute-start(bf16[1920,128]{1,0:T(8,128)(2,1)S(1)} %collective-permute-done.14.first), channel_id=1, source_target_pairs={{0,4},{1,2},{4,8},{5,1},{8,12},{9,5},{12,15},{13,9},{15,11},{14,13... | collective-permute-start | bytes 1474568 | tf_op jit(solution)/shard_map/ppermute | solution.py:301
  62.9 2.3 %shard_map.56 = (f32[1792,128]{1,0:T(8,128)S(1)}, f32[1792,128]{1,0:T(8,128)S(1)}, bf16[1792,7168]{1,0:T(8,128)(2,1)S(1)}) custom-call(bf16[1920,128]{1,0:T(8,128)(2,1)S(1)} %get-tuple-element.113.first, bf16[1920,128]{1,0:T(8,128)(2,1)S(1)} %collective-permute-done.16.second, ...), custom_call_target="tpu_custom_call", output_to_operand_aliasing={{2}: (3, {})} | custom-call | flops 1644167168 | bytes 6422528 | tf_op jit(solution)/shard_map/pallas_call | solution.py:256
  65.7 2.4 %collective-permute-start.19 = (bf16[1920,128]{1,0:T(8,128)(2,1)S(1)}, bf16[1920,128]{1,0:T(8,128)(2,1)S(1)}, u32[]{:S(2)}, u32[]{:S(2)}) collective-permute-start(bf16[1920,128]{1,0:T(8,128)(2,1)S(1)} %collective-permute-done.17.second), channel_id=1, source_target_pairs={{0,4},{1,2},{4,8},{5,1},{8,12},{9,5},{12,15},{13,9},{15,11},{14,13... | collective-permute-start | bytes 1474568 | tf_op jit(solution)/shard_map/ppermute | solution.py:304
  70.9 2.5 %collective-permute-start.18 = (bf16[1920,128]{1,0:T(8,128)(2,1)S(1)}, bf16[1920,128]{1,0:T(8,128)(2,1)S(1)}, u32[]{:S(2)}, u32[]{:S(2)}) collective-permute-start(bf16[1920,128]{1,0:T(8,128)(2,1)S(1)} %collective-permute-done.15.first), channel_id=1, source_target_pairs={{0,4},{1,2},{4,8},{5,1},{8,12},{9,5},{12,15},{13,9},{15,11},{14,13... | collective-permute-start | bytes 1474568 | tf_op jit(solution)/shard_map/ppermute | solution.py:301
  76.2 2.5 %collective-permute-start.24 = (bf16[1920,128]{1,0:T(8,128)(2,1)S(1)}, bf16[1920,128]{1,0:T(8,128)(2,1)S(1)}, u32[]{:S(2)}, u32[]{:S(2)}) collective-permute-start(bf16[1920,128]{1,0:T(8,128)(2,1)S(1)} %collective-permute-done.19.second), channel_id=1, source_target_pairs={{0,4},{1,2},{4,8},{5,1},{8,12},{9,5},{12,15},{13,9},{15,11},{14,13... | collective-permute-start | bytes 1474568 | tf_op jit(solution)/shard_map/ppermute | solution.py:304
  81.5 2.5 %collective-permute-start.22 = (bf16[1920,128]{1,0:T(8,128)(2,1)S(1)}, bf16[1920,128]{1,0:T(8,128)(2,1)S(1)}, u32[]{:S(2)}, u32[]{:S(2)}) collective-permute-start(bf16[1920,128]{1,0:T(8,128)(2,1)S(1)} %collective-permute-done.18.first), channel_id=1, source_target_pairs={{0,4},{1,2},{4,8},{5,1},{8,12},{9,5},{12,15},{13,9},{15,11},{14,13... | collective-permute-start | bytes 1474568 | tf_op jit(solution)/shard_map/ppermute | solution.py:311
  83.9 2.8 %collective-permute-done.24.second = bf16[1920,128]{1,0:T(8,128)(2,1)S(1)} collective-permute-done((bf16[1920,128]{1,0:T(8,128)(2,1)S(1)}, bf16[1920,128]{1,0:T(8,128)(2,1)S(1)}, u32[]{:S(2)}, u32[]{:S(2)}) %collective-permute-start.24) | collective-permute-done | bytes 491552 | tf_op jit(solution)/shard_map/ppermute | solution.py:304
  88.6 3.4 %collective-permute-done.22.first = bf16[1920,128]{1,0:T(8,128)(2,1)S(1)} collective-permute-done((bf16[1920,128]{1,0:T(8,128)(2,1)S(1)}, bf16[1920,128]{1,0:T(8,128)(2,1)S(1)}, u32[]{:S(2)}, u32[]{:S(2)}) %collective-permute-start.22) | collective-permute-done | bytes 491552 | tf_op jit(solution)/shard_map/ppermute | solution.py:311
  93.9 2.3 %collective-permute-start.27 = (f32[1792,128]{1,0:T(8,128)S(1)}, f32[1792,128]{1,0:T(8,128)S(1)}, u32[]{:S(2)}, u32[]{:S(2)}) collective-permute-start(f32[1792,128]{1,0:T(8,128)S(1)} %get-tuple-element.142), channel_id=1, source_target_pairs={{0,1},{1,0},{2,3},{3,2},{4,5},{5,4},{6,7},{7,6},{8,9},{9,8},{10,11... | collective-permute-start | bytes 2752520 | tf_op jit(solution)/shard_map/ppermute | solution.py:22
  98.6 3.9 %collective-permute-start.28 = (f32[8,128]{1,0:T(8,128)S(1)}, f32[8,128]{1,0:T(8,128)S(1)}, u32[]{:S(2)}, u32[]{:S(2)}) collective-permute-start(f32[8,128]{1,0:T(8,128)S(1)} %get-tuple-element.143), channel_id=1, source_target_pairs={{0,8},{1,9},{2,10},{3,11},{4,12},{5,13},{6,14},{7,15},{8,0},{9,1},... | collective-permute-start | bytes 12296 | tf_op jit(solution)/shard_map/ppermute | solution.py:29
  (71 shorter events, 47.4 us)
Async XLA Ops:
  3.9 9.1 %collective-permute-start = (bf16[1920,128]{1,0:T(8,128)(2,1)S(1)}, bf16[1920,128]{1,0:T(8,128)(2,1)S(1)}, u32[]{:S(2)}, u32[]{:S(2)}) collective-permute-start(bf16[1920,128]{1,0:T(8,128)(2,1)S(1)} %get-tuple-element.76.first), channel_id=1, source_target_pairs={{0,4},{1,2},{4,8},{5,1},{8,12},{9,5},{12,15},{13,9},{15,11},{14,13... | collective-permute-start | bytes 1474568 | tf_op jit(solution)/shard_map/ppermute | solution.py:301
  9.5 9.0 %collective-permute-start.3 = (bf16[1920,128]{1,0:T(8,128)(2,1)S(1)}, bf16[1920,128]{1,0:T(8,128)(2,1)S(1)}, u32[]{:S(2)}, u32[]{:S(2)}) collective-permute-start(bf16[1920,128]{1,0:T(8,128)(2,1)S(1)} %get-tuple-element.78.second), channel_id=1, source_target_pairs={{0,4},{1,2},{4,8},{5,1},{8,12},{9,5},{12,15},{13,9},{15,11},{14,13... | collective-permute-start | bytes 1474568 | tf_op jit(solution)/shard_map/ppermute | solution.py:304
  13.0 10.6 %collective-permute-start.2 = (bf16[1920,128]{1,0:T(8,128)(2,1)S(1)}, bf16[1920,128]{1,0:T(8,128)(2,1)S(1)}, u32[]{:S(2)}, u32[]{:S(2)}) collective-permute-start(bf16[1920,128]{1,0:T(8,128)(2,1)S(1)} %collective-permute-done.first), channel_id=1, source_target_pairs={{0,4},{1,2},{4,8},{5,1},{8,12},{9,5},{12,15},{13,9},{15,11},{14,13... | collective-permute-start | bytes 1474568 | tf_op jit(solution)/shard_map/ppermute | solution.py:301
  18.4 5.2 %collective-permute-start.6 = (bf16[1920,128]{1,0:T(8,128)(2,1)S(1)}, bf16[1920,128]{1,0:T(8,128)(2,1)S(1)}, u32[]{:S(2)}, u32[]{:S(2)}) collective-permute-start(bf16[1920,128]{1,0:T(8,128)(2,1)S(1)} %collective-permute-done.first), channel_id=1, source_target_pairs={{0,1},{1,0},{2,3},{3,2},{4,5},{5,4},{6,7},{7,6},{8,9},{9,8},{10,11... | collective-permute-start | bytes 1474568 | tf_op jit(solution)/shard_map/ppermute | solution.py:22
  18.5 7.4 %collective-permute-start.7 = (bf16[1920,128]{1,0:T(8,128)(2,1)S(1)}, bf16[1920,128]{1,0:T(8,128)(2,1)S(1)}, u32[]{:S(2)}, u32[]{:S(2)}) collective-permute-start(bf16[1920,128]{1,0:T(8,128)(2,1)S(1)} %collective-permute-done.3.second), channel_id=1, source_target_pairs={{0,1},{1,0},{2,3},{3,2},{4,5},{5,4},{6,7},{7,6},{8,9},{9,8},{10,11... | collective-permute-start | bytes 1474568 | tf_op jit(solution)/shard_map/ppermute | solution.py:22
  19.0 9.8 %collective-permute-start.5 = (bf16[1920,128]{1,0:T(8,128)(2,1)S(1)}, bf16[1920,128]{1,0:T(8,128)(2,1)S(1)}, u32[]{:S(2)}, u32[]{:S(2)}) collective-permute-start(bf16[1920,128]{1,0:T(8,128)(2,1)S(1)} %collective-permute-done.3.second), channel_id=1, source_target_pairs={{0,4},{1,2},{4,8},{5,1},{8,12},{9,5},{12,15},{13,9},{15,11},{14,13... | collective-permute-start | bytes 1474568 | tf_op jit(solution)/shard_map/ppermute | solution.py:304
  23.6 10.5 %collective-permute-start.4 = (bf16[1920,128]{1,0:T(8,128)(2,1)S(1)}, bf16[1920,128]{1,0:T(8,128)(2,1)S(1)}, u32[]{:S(2)}, u32[]{:S(2)}) collective-permute-start(bf16[1920,128]{1,0:T(8,128)(2,1)S(1)} %collective-permute-done.2.first), channel_id=1, source_target_pairs={{0,4},{1,2},{4,8},{5,1},{8,12},{9,5},{12,15},{13,9},{15,11},{14,13... | collective-permute-start | bytes 1474568 | tf_op jit(solution)/shard_map/ppermute | solution.py:301
  28.8 10.5 %collective-permute-start.10 = (bf16[1920,128]{1,0:T(8,128)(2,1)S(1)}, bf16[1920,128]{1,0:T(8,128)(2,1)S(1)}, u32[]{:S(2)}, u32[]{:S(2)}) collective-permute-start(bf16[1920,128]{1,0:T(8,128)(2,1)S(1)} %collective-permute-done.5.second), channel_id=1, source_target_pairs={{0,4},{1,2},{4,8},{5,1},{8,12},{9,5},{12,15},{13,9},{15,11},{14,13... | collective-permute-start | bytes 1474568 | tf_op jit(solution)/shard_map/ppermute | solution.py:304
  34.1 5.5 %collective-permute-start.9 = (bf16[1920,128]{1,0:T(8,128)(2,1)S(1)}, bf16[1920,128]{1,0:T(8,128)(2,1)S(1)}, u32[]{:S(2)}, u32[]{:S(2)}) collective-permute-start(bf16[1920,128]{1,0:T(8,128)(2,1)S(1)} %collective-permute-done.4.first), channel_id=1, source_target_pairs={{0,1},{1,0},{2,3},{3,2},{4,5},{5,4},{6,7},{7,6},{8,9},{9,8},{10,11... | collective-permute-start | bytes 1474568 | tf_op jit(solution)/shard_map/ppermute | solution.py:22
  34.3 10.3 %collective-permute-start.8 = (bf16[1920,128]{1,0:T(8,128)(2,1)S(1)}, bf16[1920,128]{1,0:T(8,128)(2,1)S(1)}, u32[]{:S(2)}, u32[]{:S(2)}) collective-permute-start(bf16[1920,128]{1,0:T(8,128)(2,1)S(1)} %collective-permute-done.4.first), channel_id=1, source_target_pairs={{0,4},{1,2},{4,8},{5,1},{8,12},{9,5},{12,15},{13,9},{15,11},{14,13... | collective-permute-start | bytes 1474568 | tf_op jit(solution)/shard_map/ppermute | solution.py:311
  46.5 4.4 %collective-permute-start.13 = (f32[1792,128]{1,0:T(8,128)S(1)}, f32[1792,128]{1,0:T(8,128)S(1)}, u32[]{:S(2)}, u32[]{:S(2)}) collective-permute-start(f32[1792,128]{1,0:T(8,128)S(1)} %get-tuple-element.109), channel_id=1, source_target_pairs={{0,1},{1,0},{2,3},{3,2},{4,5},{5,4},{6,7},{7,6},{8,9},{9,8},{10,11... | collective-permute-start | bytes 2752520 | tf_op jit(solution)/shard_map/ppermute | solution.py:22
  51.7 8.6 %collective-permute-start.14 = (bf16[1920,128]{1,0:T(8,128)(2,1)S(1)}, bf16[1920,128]{1,0:T(8,128)(2,1)S(1)}, u32[]{:S(2)}, u32[]{:S(2)}) collective-permute-start(bf16[1920,128]{1,0:T(8,128)(2,1)S(1)} %get-tuple-element.113.first), channel_id=1, source_target_pairs={{0,4},{1,2},{4,8},{5,1},{8,12},{9,5},{12,15},{13,9},{15,11},{14,13... | collective-permute-start | bytes 1474568 | tf_op jit(solution)/shard_map/ppermute | solution.py:301
  54.0 11.6 %collective-permute-start.17 = (bf16[1920,128]{1,0:T(8,128)(2,1)S(1)}, bf16[1920,128]{1,0:T(8,128)(2,1)S(1)}, u32[]{:S(2)}, u32[]{:S(2)}) collective-permute-start(bf16[1920,128]{1,0:T(8,128)(2,1)S(1)} %collective-permute-done.16.second), channel_id=1, source_target_pairs={{0,4},{1,2},{4,8},{5,1},{8,12},{9,5},{12,15},{13,9},{15,11},{14,13... | collective-permute-start | bytes 1474568 | tf_op jit(solution)/shard_map/ppermute | solution.py:304
  60.4 10.5 %collective-permute-start.15 = (bf16[1920,128]{1,0:T(8,128)(2,1)S(1)}, bf16[1920,128]{1,0:T(8,128)(2,1)S(1)}, u32[]{:S(2)}, u32[]{:S(2)}) collective-permute-start(bf16[1920,128]{1,0:T(8,128)(2,1)S(1)} %collective-permute-done.14.first), channel_id=1, source_target_pairs={{0,4},{1,2},{4,8},{5,1},{8,12},{9,5},{12,15},{13,9},{15,11},{14,13... | collective-permute-start | bytes 1474568 | tf_op jit(solution)/shard_map/ppermute | solution.py:301
  65.1 8.3 %collective-permute-start.20 = (bf16[1920,128]{1,0:T(8,128)(2,1)S(1)}, bf16[1920,128]{1,0:T(8,128)(2,1)S(1)}, u32[]{:S(2)}, u32[]{:S(2)}) collective-permute-start(bf16[1920,128]{1,0:T(8,128)(2,1)S(1)} %collective-permute-done.14.first), channel_id=1, source_target_pairs={{0,1},{1,0},{2,3},{3,2},{4,5},{5,4},{6,7},{7,6},{8,9},{9,8},{10,11... | collective-permute-start | bytes 1474568 | tf_op jit(solution)/shard_map/ppermute | solution.py:22
  65.7 7.8 %collective-permute-start.21 = (bf16[1920,128]{1,0:T(8,128)(2,1)S(1)}, bf16[1920,128]{1,0:T(8,128)(2,1)S(1)}, u32[]{:S(2)}, u32[]{:S(2)}) collective-permute-start(bf16[1920,128]{1,0:T(8,128)(2,1)S(1)} %collective-permute-done.17.second), channel_id=1, source_target_pairs={{0,1},{1,0},{2,3},{3,2},{4,5},{5,4},{6,7},{7,6},{8,9},{9,8},{10,11... | collective-permute-start | bytes 1474568 | tf_op jit(solution)/shard_map/ppermute | solution.py:22
  65.7 10.5 %collective-permute-start.19 = (bf16[1920,128]{1,0:T(8,128)(2,1)S(1)}, bf16[1920,128]{1,0:T(8,128)(2,1)S(1)}, u32[]{:S(2)}, u32[]{:S(2)}) collective-permute-start(bf16[1920,128]{1,0:T(8,128)(2,1)S(1)} %collective-permute-done.17.second), channel_id=1, source_target_pairs={{0,4},{1,2},{4,8},{5,1},{8,12},{9,5},{12,15},{13,9},{15,11},{14,13... | collective-permute-start | bytes 1474568 | tf_op jit(solution)/shard_map/ppermute | solution.py:304
  70.9 10.5 %collective-permute-start.18 = (bf16[1920,128]{1,0:T(8,128)(2,1)S(1)}, bf16[1920,128]{1,0:T(8,128)(2,1)S(1)}, u32[]{:S(2)}, u32[]{:S(2)}) collective-permute-start(bf16[1920,128]{1,0:T(8,128)(2,1)S(1)} %collective-permute-done.15.first), channel_id=1, source_target_pairs={{0,4},{1,2},{4,8},{5,1},{8,12},{9,5},{12,15},{13,9},{15,11},{14,13... | collective-permute-start | bytes 1474568 | tf_op jit(solution)/shard_map/ppermute | solution.py:301
  76.2 10.5 %collective-permute-start.24 = (bf16[1920,128]{1,0:T(8,128)(2,1)S(1)}, bf16[1920,128]{1,0:T(8,128)(2,1)S(1)}, u32[]{:S(2)}, u32[]{:S(2)}) collective-permute-start(bf16[1920,128]{1,0:T(8,128)(2,1)S(1)} %collective-permute-done.19.second), channel_id=1, source_target_pairs={{0,4},{1,2},{4,8},{5,1},{8,12},{9,5},{12,15},{13,9},{15,11},{14,13... | collective-permute-start | bytes 1474568 | tf_op jit(solution)/shard_map/ppermute | solution.py:304
  81.5 5.3 %collective-permute-start.23 = (bf16[1920,128]{1,0:T(8,128)(2,1)S(1)}, bf16[1920,128]{1,0:T(8,128)(2,1)S(1)}, u32[]{:S(2)}, u32[]{:S(2)}) collective-permute-start(bf16[1920,128]{1,0:T(8,128)(2,1)S(1)} %collective-permute-done.18.first), channel_id=1, source_target_pairs={{0,1},{1,0},{2,3},{3,2},{4,5},{5,4},{6,7},{7,6},{8,9},{9,8},{10,11... | collective-permute-start | bytes 1474568 | tf_op jit(solution)/shard_map/ppermute | solution.py:22
  81.5 10.5 %collective-permute-start.22 = (bf16[1920,128]{1,0:T(8,128)(2,1)S(1)}, bf16[1920,128]{1,0:T(8,128)(2,1)S(1)}, u32[]{:S(2)}, u32[]{:S(2)}) collective-permute-start(bf16[1920,128]{1,0:T(8,128)(2,1)S(1)} %collective-permute-done.18.first), channel_id=1, source_target_pairs={{0,4},{1,2},{4,8},{5,1},{8,12},{9,5},{12,15},{13,9},{15,11},{14,13... | collective-permute-start | bytes 1474568 | tf_op jit(solution)/shard_map/ppermute | solution.py:311
  93.9 4.4 %collective-permute-start.27 = (f32[1792,128]{1,0:T(8,128)S(1)}, f32[1792,128]{1,0:T(8,128)S(1)}, u32[]{:S(2)}, u32[]{:S(2)}) collective-permute-start(f32[1792,128]{1,0:T(8,128)S(1)} %get-tuple-element.142), channel_id=1, source_target_pairs={{0,1},{1,0},{2,3},{3,2},{4,5},{5,4},{6,7},{7,6},{8,9},{9,8},{10,11... | collective-permute-start | bytes 2752520 | tf_op jit(solution)/shard_map/ppermute | solution.py:22
  98.6 5.4 %collective-permute-start.28 = (f32[8,128]{1,0:T(8,128)S(1)}, f32[8,128]{1,0:T(8,128)S(1)}, u32[]{:S(2)}, u32[]{:S(2)}) collective-permute-start(f32[8,128]{1,0:T(8,128)S(1)} %get-tuple-element.143), channel_id=1, source_target_pairs={{0,8},{1,9},{2,10},{3,11},{4,12},{5,13},{6,14},{7,15},{8,0},{9,1},... | collective-permute-start | bytes 12296 | tf_op jit(solution)/shard_map/ppermute | solution.py:29
  104.1 3.6 %collective-permute-start.29 = (f32[8,128]{1,0:T(8,128)S(1)}, f32[8,128]{1,0:T(8,128)S(1)}, u32[]{:S(2)}, u32[]{:S(2)}) collective-permute-start(f32[8,128]{1,0:T(8,128)S(1)} %add.20), channel_id=1, source_target_pairs={{0,4},{1,5},{2,6},{3,7},{4,0},{5,1},{6,2},{7,3},{8,12},{9,13},{10,... | collective-permute-start | bytes 12296 | tf_op jit(solution)/shard_map/ppermute | solution.py:29
  (11 other events, 44.2 us)
